TPU v7x, 512 devices: a whole 4x4x16 slice. The times are simulated.
512 devices in a mesh: lat: 16 (over z_lo, core), lon: 32 (over y, z_hi, x).
Axes of the slice: x: 4, y: 4, z: 16 (z_hi: 2, z_lo: 8; z = z_hi * 8 + z_lo), core: 2. Of those that a mesh axis runs over, the one named last changes fastest.
Arguments:
- fields: bfloat16 [4, 96, 384, 512], P(None, 'lat', 'lon'), may hold values from -8 to 8
- qkv_weight: bfloat16 [512, 1536], replicated
- out_weight: bfloat16 [512, 512], replicated, may hold values from -0.75 to 0.75
- cotangent: bfloat16 [4, 96, 384, 512], P(None, 'lat', 'lon'), may hold values from -6 to 6
Outputs:
- layer_out: bfloat16 [4, 96, 384, 512], P(None, 'lat', 'lon')
- grad_fields: bfloat16 [4, 96, 384, 512], P(None, 'lat', 'lon')
- grad_out_weight: float32 [512, 512], P('lat', 'lon')
All inputs are finite; a program needn't handle non-finite values.
Results may differ from a plain program's by a relative error of at most 0.017.
The roundings to bfloat16 on the way count: a program that leaves them out, or rounds other values in their place, can miss the bound.
Values may be sent and summed in bfloat16 or wider, within the bound.
A program may use at most 64 MiB of HBM per device.

v0:
```python
import math

import jax
import jax.numpy as jnp
from jax import lax
from jax.sharding import PartitionSpec as P

HEAD_DIM = 64
WLEV = 2
WLAT = 6
WLON = 12


EPSILON = 1e-05
MASK_FILL = -1e30


def from_behind(value, axis, steps):
    count = lax.axis_size(axis)
    pairs = [(source, (source + steps) % count) for source in range(count)]
    return lax.ppermute(value, axis, pairs)


def normalize(fields):
    widened = fields.astype(jnp.float32)
    centred = widened - jnp.mean(widened, -1, keepdims=True)
    inverse = lax.rsqrt(jnp.mean(centred * centred, -1, keepdims=True) + EPSILON)
    normed_hat = centred * inverse
    return (normed_hat.astype(jnp.bfloat16), normed_hat, inverse)


def normalize_back(grad_normed, normed_hat, inverse):
    widened = grad_normed.astype(jnp.float32)
    centred = widened - jnp.mean(widened, -1, keepdims=True)
    return inverse * (centred - normed_hat * jnp.mean(widened * normed_hat, -1, keepdims=True))


def to_windows(blocks):
    lev_count, lat_rows, lon_cols, channels = blocks.shape
    tiled = blocks.reshape(
        lev_count // WLEV, WLEV, lat_rows // WLAT, WLAT, lon_cols // WLON, WLON, channels
    )
    return tiled.transpose(0, 2, 4, 1, 3, 5, 6).reshape(-1, WLEV * WLAT * WLON, channels)


def from_windows(windows, grid_shape):
    lev_count, lat_rows, lon_cols, channels = grid_shape
    tiled = windows.reshape(
        lev_count // WLEV, lat_rows // WLAT, lon_cols // WLON, WLEV, WLAT, WLON, channels
    )
    return tiled.transpose(0, 3, 1, 4, 2, 5, 6).reshape(grid_shape)


def region_ids(lev_count, lat_global, lat_total, lon_cols):
    levels = jnp.arange(lev_count, dtype=jnp.int32)
    lev_region = (levels >= lev_count - WLEV).astype(jnp.int32) + (
        levels >= lev_count - WLEV // 2
    ).astype(jnp.int32)
    lat_region = (lat_global >= lat_total - WLAT).astype(jnp.int32) + (
        lat_global >= lat_total - WLAT // 2
    ).astype(jnp.int32)
    return (
        3 * lev_region[:, None, None]
        + lat_region[None, :, None]
        + jnp.zeros((1, 1, lon_cols), jnp.int32)
    )


def window_forward(windows, allowed, qkv_weight, out_weight):
    win_count, win_tokens, channels = windows.shape
    head_count = channels // HEAD_DIM
    projected = jnp.dot(
        windows.reshape(-1, channels), qkv_weight, preferred_element_type=jnp.float32
    ).astype(jnp.bfloat16)
    projected = projected.reshape(win_count, win_tokens, 3, head_count, HEAD_DIM)
    queries = projected[:, :, 0]
    key_rows = projected[:, :, 1]
    values = projected[:, :, 2]
    scores = jnp.einsum(
        "nqhe,nkhe->nhqk", queries, key_rows, preferred_element_type=jnp.float32
    ) * HEAD_DIM ** (-0.5)
    scores = jnp.where(allowed[:, None], scores, MASK_FILL)
    lifted = jnp.exp(scores - jnp.max(scores, -1, keepdims=True))
    attend = lifted / jnp.sum(lifted, -1, keepdims=True)
    attend_low = attend.astype(jnp.bfloat16)
    context = jnp.einsum("nhqk,nkhe->nqhe", attend_low, values, preferred_element_type=jnp.float32)
    context = context.astype(jnp.bfloat16).reshape(-1, channels)
    output = jnp.dot(context, out_weight, preferred_element_type=jnp.float32).astype(jnp.bfloat16)
    return (output, (queries, key_rows, values, attend, attend_low, context))


def window_backward(saved, grad_rows, qkv_weight, out_weight):
    queries, key_rows, values, attend, attend_low, context = saved
    channels = context.shape[1]
    grad_context = lax.dot_general(
        grad_rows, out_weight, (((1,), (1,)), ((), ())), preferred_element_type=jnp.float32
    )
    grad_context = grad_context.astype(jnp.bfloat16).reshape(queries.shape)
    grad_attend = jnp.einsum(
        "nqhe,nkhe->nhqk", grad_context, values, preferred_element_type=jnp.float32
    )
    grad_scores = (
        attend
        * (grad_attend - jnp.sum(attend * grad_attend, -1, keepdims=True))
        * HEAD_DIM ** (-0.5)
    )
    grad_scores = grad_scores.astype(jnp.bfloat16)
    grad_query = jnp.einsum(
        "nhqk,nkhe->nqhe", grad_scores, key_rows, preferred_element_type=jnp.float32
    )
    grad_keys = jnp.einsum(
        "nhqk,nqhe->nkhe", grad_scores, queries, preferred_element_type=jnp.float32
    )
    grad_values = jnp.einsum(
        "nhqk,nqhe->nkhe", attend_low, grad_context, preferred_element_type=jnp.float32
    )
    grad_proj = (
        jnp.stack([grad_query, grad_keys, grad_values], 2)
        .astype(jnp.bfloat16)
        .reshape(-1, 3 * channels)
    )
    grad_shifted = lax.dot_general(
        grad_proj, qkv_weight, (((1,), (1,)), ((), ())), preferred_element_type=jnp.float32
    )
    return grad_shifted.astype(jnp.bfloat16)


def shift_forward(blocks):
    lon_half = WLON // 2
    lat_half = WLAT // 2
    arriving = from_behind(blocks[..., :lon_half, :], "lon", -1)
    lon_shifted = jnp.concatenate([blocks[..., lon_half:, :], arriving], -2)
    rising = from_behind(lon_shifted[..., :lat_half, :, :], "lat", -1)
    lat_shifted = jnp.concatenate([lon_shifted[..., lat_half:, :, :], rising], -3)
    return jnp.roll(lat_shifted, -(WLEV // 2), axis=-4)


def shift_back(blocks):
    lon_half = WLON // 2
    lat_half = WLAT // 2
    lat_rows = blocks.shape[-3]
    lon_cols = blocks.shape[-2]
    rolled = jnp.roll(blocks, WLEV // 2, axis=-4)
    sinking = from_behind(rolled[..., lat_rows - lat_half :, :, :], "lat", 1)
    lat_shifted = jnp.concatenate([sinking, rolled[..., : lat_rows - lat_half, :, :]], -3)
    leaving = from_behind(lat_shifted[..., lon_cols - lon_half :, :], "lon", 1)
    return jnp.concatenate([leaving, lat_shifted[..., : lon_cols - lon_half, :]], -2)


def on_device(fields, qkv_weight, out_weight, cotangent):
    grid_shape = fields.shape
    lev_count, lat_rows, lon_cols, channels = grid_shape
    lat_devices = lax.axis_size("lat")
    lon_devices = lax.axis_size("lon")
    lat_total = lat_rows * lat_devices
    factor = 1.0 / math.sqrt(lev_count * lat_total * lon_cols * lon_devices)
    normed, normed_hat, inverse = normalize(fields)
    lat_global = lax.axis_index("lat") * lat_rows + jnp.arange(lat_rows, dtype=jnp.int32)
    region = region_ids(lev_count, lat_global, lat_total, lon_cols)
    region_win = to_windows(region[..., None])[..., 0]
    allowed = region_win[:, :, None] == region_win[:, None, :]
    win_tokens = WLEV * WLAT * WLON
    shifted = shift_forward(normed)
    output, saved = window_forward(to_windows(shifted), allowed, qkv_weight, out_weight)
    branch_back = shift_back(from_windows(output.reshape(-1, win_tokens, channels), grid_shape))
    shifted_cot = shift_forward(cotangent)
    grad_rows = to_windows(shifted_cot).reshape(-1, channels)
    grad_shifted = window_backward(saved, grad_rows, qkv_weight, out_weight)
    grad_normed = shift_back(
        from_windows(grad_shifted.reshape(-1, win_tokens, channels), grid_shape)
    )
    layer_out = (fields.astype(jnp.float32) + branch_back.astype(jnp.float32)).astype(jnp.bfloat16)
    grad_fields = (
        cotangent.astype(jnp.float32) + normalize_back(grad_normed, normed_hat, inverse)
    ).astype(jnp.bfloat16)
    context = saved[5]
    lat_part = lax.psum_scatter(
        lax.dot_general(
            context, grad_rows, (((0,), (0,)), ((), ())), preferred_element_type=jnp.float32
        )
        * factor,
        "lat",
        scatter_dimension=0,
        tiled=True,
    )
    grad_out_weight = lax.psum_scatter(lat_part, "lon", scatter_dimension=1, tiled=True)
    return (layer_out, grad_fields, grad_out_weight)


def solution(mesh):
    in_specs = (P(None, "lat", "lon", None), P(), P(), P(None, "lat", "lon", None))
    out_specs = (P(None, "lat", "lon", None), P(None, "lat", "lon", None), P("lat", "lon"))
    return jax.shard_map(
        on_device, mesh=mesh, in_specs=in_specs, out_specs=out_specs, check_vma=False
    )
```

profile of v0, /device:TPU:32, one launch (start us, length us, event | category | flops | bytes accessed | tf_op | source)
XLA Modules:
  0.0 523.6 jit_solution(17572200373629988116)
XLA Ops:
  11.2 19.5 %collective-permute-start = (bf16[4,6,6,512]{3,0,2,1:T(4,128)(2,1)S(1)}, bf16[4,6,6,512]{3,0,2,1:T(4,128)(2,1)S(1)}, u32[]{:S(2)}, u32[]{:S(2)}) collective-permute-start(bf16[4,6,6,512]{3,0,2,1:T(4,128)(2,1)S(1)} %get-tuple-element.30), channel_id=1, source_target_pairs={{0,31},{1,0},{2,1},{3,2},{4,3},{5,4},{6,5},{7,6},{8,7},{9,8},{10,9... | collective-permute-start | bytes 442376 | tf_op jit(solution)/shard_map/ppermute | solution.py:21
  30.8 2.7 collective-permute-start.4
  33.8 16.7 %collective-permute-done = bf16[4,6,6,512]{3,0,2,1:T(4,128)(2,1)S(1)} collective-permute-done((bf16[4,6,6,512]{3,0,2,1:T(4,128)(2,1)S(1)}, bf16[4,6,6,512]{3,0,2,1:T(4,128)(2,1)S(1)}, u32[]{:S(2)}, u32[]{:S(2)}) %collective-permute-start) | collective-permute-done | bytes 147488 | tf_op jit(solution)/shard_map/ppermute | solution.py:21
  50.7 1.9 collective-permute-start.1
  53.4 2.5 collective-permute-done.4
  56.8 2.9 collective-permute-start.5
  62.0 2.6 reshape.100
  65.9 2.3 copy.64
  68.2 2.3 copy.65
  77.1 3.0 fusion.49
  80.1 3.5 fusion.86
  83.6 3.0 fusion.18
  91.5 5.4 %fusion.23 = bf16[2,144,1,8,64]{1,4,3,0,2:T(8,128)(2,1)} fusion(f32[2,8,144,144]{2,3,1,0:T(8,128)} %fusion.49, bf16[2,144,1,8,64]{1,4,3,0,2:T(8,128)(2,1)S(1)} %copy-done.14, f32[2,8,144,144]{2,3,1,0:T(8,128)} %get-tuple-element.32, f32[2,8,144]{2,1,0:T(8,128)S(1)} %get-tuple-element.31), kind=kOutput, calls=%fused_computation.20 | convolution fusion | flops 44939664 | bytes 3253248 | tf_op jit(solution)/shard_map/nhqk,nkhe->nqhe/dot_general | solution.py:108
  96.9 5.5 %fusion.20 = bf16[2,144,1,8,64]{1,4,3,0,2:T(8,128)(2,1)} fusion(f32[2,8,144,144]{2,3,1,0:T(8,128)} %fusion.49, bf16[2,144,1,8,64]{1,4,3,0,2:T(8,128)(2,1)S(1)} %copy-done.13, f32[2,8,144,144]{2,3,1,0:T(8,128)} %get-tuple-element.32, f32[2,8,144]{2,1,0:T(8,128)S(1)} %get-tuple-element.31), kind=kOutput, calls=%fused_computation.19 | convolution fusion | flops 44939664 | bytes 3253248 | tf_op jit(solution)/shard_map/nhqk,nqhe->nkhe/dot_general | solution.py:111
  102.5 2.6 pad_maximum_fusion
  105.1 2.9 copy.53
  112.9 1.9 collective-permute-start.6
  115.7 2.1 collective-permute-start.2
  117.8 1.9 collective-permute-done.6
  120.9 1.9 collective-permute-start.7
  123.3 1.9 collective-permute-start.3
  125.2 35.1 %collective-permute-done.7 = bf16[4,6,6,512]{3,0,2,1:T(4,128)(2,1)S(1)} collective-permute-done((bf16[4,6,6,512]{3,0,2,1:T(4,128)(2,1)S(1)}, bf16[4,6,6,512]{3,0,2,1:T(4,128)(2,1)S(1)}, u32[]{:S(2)}, u32[]{:S(2)}) %collective-permute-start.7) | collective-permute-done | bytes 147488 | tf_op jit(solution)/shard_map/ppermute | solution.py:21
  160.9 29.7 %reduce-scatter.5.cloned.1.call-done = f32[32,512]{1,0:T(8,128)} async-done(((f32[512,512]{1,0:T(8,128)}), f32[32,512]{1,0:T(8,128)}) %reduce-scatter.5.cloned.1.call-update) | async-done | bytes 65552 | tf_op jit(solution)/shard_map/reduce_scatter | solution.py:177
  193.8 322.9 %reduce-scatter.7.cloned.1.call-done = f32[16,32]{1,0:T(8,128)} async-done(((f32[512,32]{1,0:T(8,128)}), f32[16,32]{1,0:T(8,128)}) %reduce-scatter.7.cloned.1.call-update) | async-done | bytes 2064
  (102 shorter events, 32.2 us)
Async XLA Ops:
  7.2 53.3 %copy-start = (bf16[512,1536]{1,0:T(8,128)(2,1)S(1)}, bf16[512,1536]{1,0:T(8,128)(2,1)}, u32[]{:S(2)}) copy-start(bf16[512,1536]{1,0:T(8,128)(2,1)} %param.5) | copy-start | bytes 4718596
  7.2 23.5 %copy-start.8 = (bf16[4,6,12,512]{3,0,2,1:T(4,128)(2,1)S(1)}, bf16[4,6,12,512]{3,0,2,1:T(4,128)(2,1)}, u32[]{:S(2)}) copy-start(bf16[4,6,12,512]{3,0,2,1:T(4,128)(2,1)} %param.7) | copy-start | bytes 884740
  7.2 183.5 %reduce-scatter.5.cloned.1.call-start = ((), (), s32[]{:S(2)}) async-start(), calls=%async_computation.2 | async-start | bytes 1114112 | tf_op jit(solution)/shard_map/reduce_scatter | solution.py:177
  9.9 49.9 %copy-start.10 = (f32[4,6,12]{0,2,1:T(8,128)}, f32[4,6,12]{0,2,1:T(8,128)S(1)}, u32[]{:S(2)}) copy-start(f32[4,6,12]{0,2,1:T(8,128)S(1)} %add_rsqrt_fusion) | copy-start | bytes 3460
  11.2 39.3 %collective-permute-start = (bf16[4,6,6,512]{3,0,2,1:T(4,128)(2,1)S(1)}, bf16[4,6,6,512]{3,0,2,1:T(4,128)(2,1)S(1)}, u32[]{:S(2)}, u32[]{:S(2)}) collective-permute-start(bf16[4,6,6,512]{3,0,2,1:T(4,128)(2,1)S(1)} %get-tuple-element.30), channel_id=1, source_target_pairs={{0,31},{1,0},{2,1},{3,2},{4,3},{5,4},{6,5},{7,6},{8,7},{9,8},{10,9... | collective-permute-start | bytes 442376 | tf_op jit(solution)/shard_map/ppermute | solution.py:21
  30.8 25.1 %collective-permute-start.4 = (bf16[4,6,6,512]{3,0,2,1:T(4,128)(2,1)S(1)}, bf16[4,6,6,512]{3,0,2,1:T(4,128)(2,1)S(1)}, u32[]{:S(2)}, u32[]{:S(2)}) collective-permute-start(bf16[4,6,6,512]{3,0,2,1:T(4,128)(2,1)S(1)} %get-tuple-element.24), channel_id=1, source_target_pairs={{0,31},{1,0},{2,1},{3,2},{4,3},{5,4},{6,5},{7,6},{8,7},{9,8},{10,9... | collective-permute-start | bytes 442376 | tf_op jit(solution)/shard_map/ppermute | solution.py:21
  50.7 9.0 %collective-permute-start.1 = (bf16[4,3,12,512]{3,0,2,1:T(4,128)(2,1)S(1)}, bf16[4,3,12,512]{3,0,2,1:T(4,128)(2,1)S(1)}, u32[]{:S(2)}, u32[]{:S(2)}) collective-permute-start(bf16[4,3,12,512]{3,0,2,1:T(4,128)(2,1)S(1)} %get-tuple-element.28), channel_id=1, source_target_pairs={{0,480},{32,0},{64,32},{96,64},{128,96},{160,128},{192,160},{224,1... | collective-permute-start | bytes 442376 | tf_op jit(solution)/shard_map/ppermute | solution.py:21
  56.8 14.1 %collective-permute-start.5 = (bf16[4,3,12,512]{3,0,2,1:T(4,128)(2,1)}, bf16[4,3,12,512]{3,0,2,1:T(4,128)(2,1)}, u32[]{:S(2)}, u32[]{:S(2)}) collective-permute-start(bf16[4,3,12,512]{3,0,2,1:T(4,128)(2,1)} %get-tuple-element.22), channel_id=1, source_target_pairs={{0,480},{32,0},{64,32},{96,64},{128,96},{160,128},{192,160},{224,1... | collective-permute-start | bytes 442376 | tf_op jit(solution)/shard_map/ppermute | solution.py:21
  65.9 4.6 copy-start.4
  68.2 7.0 %copy-start.5 = (bf16[512,512]{1,0:T(8,128)(2,1)S(1)}, bf16[512,512]{1,0:T(8,128)(2,1)}, u32[]{:S(2)}) copy-start(bf16[512,512]{1,0:T(8,128)(2,1)} %param.6) | copy-start | bytes 1572868
  89.7 7.2 %copy-start.2 = (bf16[288,512]{1,0:T(8,128)(2,1)}, bf16[288,512]{1,0:T(8,128)(2,1)S(1)}, u32[]{:S(2)}) copy-start(bf16[288,512]{1,0:T(8,128)(2,1)S(1)} %reshape.101) | copy-start | bytes 884740
  91.2 5.7 %copy-start.13 = (bf16[2,144,1,8,64]{1,4,3,0,2:T(8,128)(2,1)S(1)}, bf16[2,144,1,8,64]{1,4,3,0,2:T(8,128)(2,1)}, u32[]{:S(2)}) copy-start(bf16[2,144,1,8,64]{1,4,3,0,2:T(8,128)(2,1)} %copy.64) | copy-start | bytes 884740
  91.2 425.5 %reduce-scatter.7.cloned.1.call-start = ((), (), s32[]{:S(2)}) async-start(), calls=%async_computation.3 | async-start | bytes 270336
  96.9 5.6 %copy-start.15 = (bf16[2,144,1,8,64]{1,4,3,0,2:T(8,128)(2,1)S(1)}, bf16[2,144,1,8,64]{1,4,3,0,2:T(8,128)(2,1)}, u32[]{:S(2)}) copy-start(bf16[2,144,1,8,64]{1,4,3,0,2:T(8,128)(2,1)} %fusion.19) | copy-start | bytes 884740
  96.9 5.6 %copy-start.16 = (bf16[2,144,1,8,64]{1,4,3,0,2:T(8,128)(2,1)S(1)}, bf16[2,144,1,8,64]{1,4,3,0,2:T(8,128)(2,1)}, u32[]{:S(2)}) copy-start(bf16[2,144,1,8,64]{1,4,3,0,2:T(8,128)(2,1)} %fusion.23) | copy-start | bytes 884740
  109.8 5.0 copy-start.3
  109.8 5.0 copy-start.6
  112.9 6.8 %collective-permute-start.6 = (bf16[4,3,12,512]{3,0,2,1:T(4,128)(2,1)}, bf16[4,3,12,512]{3,0,2,1:T(4,128)(2,1)}, u32[]{:S(2)}, u32[]{:S(2)}) collective-permute-start(bf16[4,3,12,512]{3,0,2,1:T(4,128)(2,1)} %fusion.64), channel_id=1, source_target_pairs={{0,32},{32,64},{64,96},{96,128},{128,160},{160,192},{192,224},{224... | collective-permute-start | bytes 442376 | tf_op jit(solution)/shard_map/ppermute | solution.py:21
  115.2 45.1 %copy-start.1 = (bf16[4,6,12,512]{3,0,2,1:T(4,128)(2,1)S(1)}, bf16[4,6,12,512]{3,0,2,1:T(4,128)(2,1)}, u32[]{:S(2)}) copy-start(bf16[4,6,12,512]{3,0,2,1:T(4,128)(2,1)} %param.4) | copy-start | bytes 884740
  115.2 45.1 %copy-start.11 = (f32[4,6,12]{0,2,1:T(8,128)S(1)}, f32[4,6,12]{0,2,1:T(8,128)}, u32[]{:S(2)}) copy-start(f32[4,6,12]{0,2,1:T(8,128)} %copy-done.10) | copy-start | bytes 3460
  115.7 76.7 %copy-start.9 = (bf16[4,6,12,512]{3,0,2,1:T(4,128)(2,1)S(1)}, bf16[4,6,12,512]{3,0,2,1:T(4,128)(2,1)}, u32[]{:S(2)}) copy-start(bf16[4,6,12,512]{3,0,2,1:T(4,128)(2,1)} %param.7) | copy-start | bytes 884740
  115.7 7.2 %collective-permute-start.2 = (bf16[4,3,12,512]{3,0,2,1:T(4,128)(2,1)S(1)}, bf16[4,3,12,512]{3,0,2,1:T(4,128)(2,1)S(1)}, u32[]{:S(2)}, u32[]{:S(2)}) collective-permute-start(bf16[4,3,12,512]{3,0,2,1:T(4,128)(2,1)S(1)} %fusion.66), channel_id=1, source_target_pairs={{0,32},{32,64},{64,96},{96,128},{128,160},{160,192},{192,224},{224... | collective-permute-start | bytes 442376 | tf_op jit(solution)/shard_map/ppermute | solution.py:21
  120.9 39.4 %collective-permute-start.7 = (bf16[4,6,6,512]{3,0,2,1:T(4,128)(2,1)S(1)}, bf16[4,6,6,512]{3,0,2,1:T(4,128)(2,1)S(1)}, u32[]{:S(2)}, u32[]{:S(2)}) collective-permute-start(bf16[4,6,6,512]{3,0,2,1:T(4,128)(2,1)S(1)} %get-tuple-element.19), channel_id=1, source_target_pairs={{0,1},{1,2},{2,3},{3,4},{4,5},{5,6},{6,7},{7,8},{8,9},{9,10},{10,1... | collective-permute-start | bytes 442376 | tf_op jit(solution)/shard_map/ppermute | solution.py:21
  123.3 69.1 %collective-permute-start.3 = (bf16[4,6,6,512]{3,0,2,1:T(4,128)(2,1)S(1)}, bf16[4,6,6,512]{3,0,2,1:T(4,128)(2,1)S(1)}, u32[]{:S(2)}, u32[]{:S(2)}) collective-permute-start(bf16[4,6,6,512]{3,0,2,1:T(4,128)(2,1)S(1)} %get-tuple-element.25), channel_id=1, source_target_pairs={{0,1},{1,2},{2,3},{3,4},{4,5},{5,6},{6,7},{7,8},{8,9},{9,10},{10,1... | collective-permute-start | bytes 442376 | tf_op jit(solution)/shard_map/ppermute | solution.py:21
  (5 other events, 16.8 us)
Sparse Core Ops, SparseCore 0:
  91.4 99.2 reduce-scatter.4
  194.3 322.4 reduce-scatter.6
where the time goes:
time: 524 us
  waiting for transfers between devices  409 us (78%)
  starting transfers between devices  35.1 us (7%)
  matrix products  27.4 us (5%)
  local copies, waits for them, and re-layouts  21.9 us (4%)
  other arithmetic  15.6 us (3%)
  between operations  14.6 us (3%)
    unnamed x3, waiting for transfers between devices  323 us
    ppermute x8, waiting for transfers between devices, from_behind(): return lax.ppermute(value, axis, pairs)  56.3 us
    ppermute x8, starting transfers between devices, from_behind(): return lax.ppermute(value, axis, pairs)  34.8 us
    reduce_scatter x1, waiting for transfers between devices, on_device(): lax.psum_scatter(lax.dot_general(context, grad_rows, (((0,), (0,)), ((),...  29.7 us
  transfers between devices with their start and end apart: 10, of which 7 were waited for; matrix products, arithmetic and copies ran while one was open for 8% of the time, Pallas kernels for 0%

commit v1 on v0

v1 whole, which is shorter than its diff:
```python
import functools
import math

import jax
import jax.numpy as jnp
from jax import lax
from jax.experimental import pallas as pl
from jax.experimental.pallas import tpu as pltpu
from jax.sharding import PartitionSpec as P

MESH = pl.DeviceIdType.MESH
EPSILON = 1e-05
MASK_FILL = -1e30
BF = jnp.bfloat16
F32 = jnp.float32
D = 512
LATS = 16
LONS = 32
BLOCK = (16, 1152)


def dot(a, b, ca=1, cb=0):
    return lax.dot_general(a, b, (((ca,), (cb,)), ((), ())), preferred_element_type=F32)


def iota(shape, dim):
    return lax.broadcasted_iota(jnp.int32, shape, dim)


def ones_where(cond):
    return jnp.where(cond, 1.0, 0.0).astype(BF)


def z_quarter(lat, lon, back):
    zl = lat // 2
    h = (lon // 4) % 2
    low = (zl + 4) % 8
    wraps = 1 - zl // 4 if back else zl // 4
    return low * 2 + lat % 2, lon + ((h + wraps) % 2 - h) * 4


def moved(lat, lon, cond, back):
    qlat, qlon = z_quarter(lat, lon, back)
    return jnp.where(cond, qlat, lat), jnp.where(cond, qlon, lon)


def block_host(lat, lon, r, c, p):
    kb = lon if c == 1 else (lon + LONS - 1) % LONS
    crossing = kb % 4 == 3
    q = (1 - r) * 2 + (1 - c)
    east = (kb + 1) % LONS
    if p == 0 and r == 1:
        hlat, hlon, pos = lat, kb, q
    elif p == 0:
        edge = lat == 0
        hlat = jnp.where(edge, 0, lat - 1)
        hlon = jnp.where(edge, east, kb)
        pos = jnp.where(edge, 4 + q - 2, q)
    elif r == 0:
        hlat, hlon, pos = lat, east, 4 + q
    else:
        edge = lat == LATS - 1
        hlat = jnp.where(edge, LATS - 1, lat + 1)
        hlon = jnp.where(edge, kb, east)
        pos = jnp.where(edge, q + 2, 4 + q)
    hlat, hlon = moved(hlat, hlon, crossing, False)
    return hlat, hlon, pos


def virtual_host(lat, lon, slot):
    x = lon % 4
    crossing = x == jnp.where(slot == 0, 3, 0)
    return moved(lat, lon, crossing, True)


def inbox_source(lat, lon, slot, q):
    va, vb = virtual_host(lat, lon, slot)
    south, east = q // 2, q % 2
    if slot == 0:
        edge = va == LATS - 1
        if south == 0:
            slat, r, p = va, 1, 0
        else:
            slat = jnp.where(edge, va, va + 1)
            r = jnp.where(edge, 1, 0)
            p = jnp.where(edge, 1, 0)
        slon = (vb + east) % LONS
    else:
        edge = va == 0
        if south == 1:
            slat, r, p = va, 0, 1
        else:
            slat = jnp.where(edge, va, va - 1)
            r = jnp.where(edge, 0, 1)
            p = jnp.where(edge, 0, 1)
        slon = (vb + LONS - 1 + east) % LONS
    return slat, slon, (r * 2 + (1 - east)) * 2 + p


def grid_row(m):
    tail = m >= 256
    k = jnp.where(tail, (m - 256) >> 2, m >> 5)
    t = jnp.where(tail, 32 + ((m - 256) & 3), m & 31)
    r, c, p = k >> 2, (k >> 1) & 1, k & 1
    l2 = jnp.where(t >= 18, 1, 0)
    t = t - 18 * l2
    r3 = jnp.where(t >= 6, 1, 0) + jnp.where(t >= 12, 1, 0)
    lev = (1 + 2 * p + l2) & 3
    return (lev * 6 + 3 * r + r3) * 16 + 6 * c + t - 6 * r3


def tail_map(count, j):
    rows = iota((4 * count, 1), 0)
    return ones_where((rows >> 2) * 16 + 4 * j + (rows & 3) == iota((4 * count, 16 * count), 1))


def store_blocks(ref, base, rows, count):
    for k in range(count):
        ref[base + k, :, 0:512] = rows[32 * k : 32 * k + 16]
        ref[base + k, :, 512:1024] = rows[32 * k + 16 : 32 * k + 32]
    tails = rows[32 * count :]
    packed = sum(
        dot(tail_map(count, j), tails[:, 128 * j : 128 * j + 128], 0, 0) for j in range(4)
    ).astype(BF)
    for k in range(count):
        ref[base + k, :, 1024:1152] = packed[16 * k : 16 * k + 16]


def load_blocks(ref, base, count):
    main = []
    for k in range(count):
        main += [ref[base + k, :, 0:512], ref[base + k, :, 512:1024]]
    packed = jnp.concatenate([ref[base + k, :, 1024:1152] for k in range(count)], 0)
    tails = jnp.concatenate([dot(tail_map(count, j), packed) for j in range(4)], 1).astype(BF)
    return jnp.concatenate(main + [tails], 0)


def group_ids(m, slot, edge):
    tail = m >= 128
    q = jnp.where(tail, (m - 128) >> 2, m >> 5)
    t = jnp.where(tail, 32 + ((m - 128) & 3), m & 31)
    l2 = jnp.where(t >= 18, 1, 0)
    south = q >> 1
    first = jnp.where(edge, south * (1 + l2), 0)
    second = jnp.where(edge, jnp.where(south == 0, 2, l2), l2)
    return jnp.where(slot == 0, first, second)


def kernel(
    factor,
    fields_ref, qkv_hbm, out_hbm, cot_ref,
    layer_ref, grad_ref, dw_ref,
    pad, hat, inv, qkv_w, out_w,
    out_f, out_c, in_f, in_c, res_b, res_g, ret_b, ret_g,
    proj, att, ctx, gproj, acc,
    a_src, a_dst, b_src, b_dst, c_src, c_dst, d_src, d_dst,
    w_sem, sf, sc, sb, sg, rf, rc, rb, rg,
    a_sem, bs_sem, br_sem, cs_sem, cr_sem, ds_sem, dr_sem,
):
    lat = lax.axis_index("lat")
    lon = lax.axis_index("lon")
    core, zl = lat % 2, lat // 2
    y, h, x = lon // 8, (lon // 4) % 2, lon % 4
    z = h * 8 + zl
    yx = y * 4 + x
    collector = zl // 2 == x

    def at(y_, x_, z_, c_):
        return ((z_ % 8) * 2 + c_, y_ * 8 + (z_ // 8) * 4 + x_)

    def same(dlat, dlon):
        return jnp.logical_and(dlat == lat, dlon == lon)

    load_w = [
        pltpu.make_async_copy(qkv_hbm, qkv_w, w_sem.at[0]),
        pltpu.make_async_copy(out_hbm, out_w, w_sem.at[1]),
    ]
    for copy in load_w:
        copy.start()

    hosts = [block_host(lat, lon, k >> 2, (k >> 1) & 1, k & 1) for k in range(8)]
    sources = [inbox_source(lat, lon, i // 4, i % 4) for i in range(8)]

    barrier = pltpu.get_barrier_semaphore()

    def tell(dlat, dlon):
        pl.semaphore_signal(barrier, inc=1, device_id=(dlat, dlon), device_id_type=MESH)

    due = jnp.int32(16)
    for slat, slon, _ in sources:
        pl.when(jnp.logical_not(same(slat, slon)))(functools.partial(tell, slat, slon))
    for hlat, hlon, _ in hosts:
        due = due + jnp.where(same(hlat, hlon), 0, 1)
    tell(zl * 2 + 1 - core, lon)

    def tell_plane(d, carry):
        partner = yx ^ d
        tell(*at(partner // 4, partner % 4, z, core))
        return carry

    lax.fori_loop(1, 16, tell_plane, 0)

    @pl.when(collector)
    def _():
        def tell_ring(d, carry):
            tell(*at(y, x, z ^ d, core))
            return carry

        lax.fori_loop(1, 16, tell_ring, 0)

    due = due + jnp.where(collector, 3, 4)

    pad[...] = jnp.zeros_like(pad)
    pad[0, :, 0:12, :] = fields_ref[...]
    pad[1, :, 0:12, :] = cot_ref[...]
    wide = pad[0].reshape(384, D).astype(F32)
    centred = wide - jnp.mean(wide, -1, keepdims=True)
    inverse = lax.rsqrt(jnp.mean(centred * centred, -1, keepdims=True) + EPSILON)
    normed_hat = centred * inverse
    hat[...] = normed_hat
    inv[...] = inverse
    to_blocks = ones_where(grid_row(iota((288, 1), 0)) == iota((288, 384), 1))
    store_blocks(out_f, 0, dot(to_blocks, normed_hat.astype(BF)).astype(BF), 8)
    store_blocks(out_c, 0, dot(to_blocks, pad[1].reshape(384, D)).astype(BF), 8)

    pl.semaphore_wait(barrier, due)

    def send(src, dst, send_sems, recv_sems, i, dlat, dlon, j):
        here = same(dlat, dlon)

        @pl.when(here)
        def _():
            pltpu.make_async_copy(src.at[i], dst.at[j], recv_sems.at[j]).start()

        @pl.when(jnp.logical_not(here))
        def _():
            pltpu.make_async_remote_copy(
                src_ref=src.at[i], dst_ref=dst.at[j], send_sem=send_sems.at[i], recv_sem=recv_sems.at[j],
                device_id=(dlat, dlon), device_id_type=MESH,
            ).start()

    def landed(dst, sems, j):
        pltpu.make_async_copy(dst.at[j], dst.at[j], sems.at[j]).wait()

    def sent(src, sems, i, dlat, dlon):
        @pl.when(jnp.logical_not(same(dlat, dlon)))
        def _():
            pltpu.make_async_copy(src.at[i], src.at[i], sems.at[i]).wait()

    for src, dst, ss, rs in ((out_f, in_f, sf, rf), (out_c, in_c, sc, rc)):
        for k, (hlat, hlon, pos) in enumerate(hosts):
            send(src, dst, ss, rs, k, hlat, hlon, pos)

    for copy in load_w:
        copy.wait()

    first_half = iota((144, 128), 1) < 64

    def halves(pair):
        zero = jnp.zeros_like(pair)
        return jnp.concatenate([jnp.where(first_half, pair, zero), jnp.where(first_half, zero, pair)], 0)

    def merge(stacked):
        return jnp.where(first_half, stacked[:144], stacked[144:])

    def send_back(slot, src, dst, ss, rs):
        for s in range(2):
            @pl.when(slot == s)
            def _():
                for q in range(4):
                    slat, slon, k = sources[s * 4 + q]
                    send(src, dst, ss, rs, s * 4 + q, slat, slon, k)

    def window(i, carry):
        slot = jnp.where(x == 0, i, 1 - i)
        va, _ = virtual_host(lat, lon, slot)
        edge = va == jnp.where(slot == 0, LATS - 1, 0)
        base = slot * 4
        for q in range(4):
            landed(in_f, rf, base + q)
        tokens = load_blocks(in_f, base, 4)
        proj[...] = dot(tokens, qkv_w[...]).astype(BF)
        allowed = group_ids(iota((144, 1), 0), slot, edge) == group_ids(iota((1, 144), 1), slot, edge)
        allowed = jnp.concatenate([allowed, allowed], 0)
        for g in range(4):
            lanes = slice(128 * g, 128 * g + 128)
            query = halves(proj[:, lanes])
            key = proj[:, 512 + 128 * g : 640 + 128 * g]
            value = proj[:, 1024 + 128 * g : 1152 + 128 * g]
            scores = jnp.where(allowed, dot(query, key, 1, 1) * 0.125, MASK_FILL)
            lifted = jnp.exp(scores - jnp.max(scores, -1, keepdims=True))
            attend = lifted * (1.0 / jnp.sum(lifted, -1, keepdims=True))
            att[g] = attend
            ctx[:, lanes] = merge(dot(attend.astype(BF), value)).astype(BF)
        store_blocks(res_b, base, dot(ctx[...], out_w[...]).astype(BF), 4)
        send_back(slot, res_b, ret_b, sb, rb)

        for q in range(4):
            landed(in_c, rc, base + q)
        cot = load_blocks(in_c, base, 4)
        term = dot(ctx[...], cot, 0, 0).reshape(8, 2, 32, D)

        @pl.when(i == 0)
        def _():
            acc[...] = term

        @pl.when(i == 1)
        def _():
            acc[...] = (acc[...] + term) * factor
            a_src[...] = acc[:, 1 - core].astype(BF)
            pltpu.make_async_remote_copy(
                src_ref=a_src, dst_ref=a_dst, send_sem=a_sem.at[0], recv_sem=a_sem.at[1],
                device_id=(zl * 2 + 1 - core, lon), device_id_type=MESH,
            ).start()

        grad_ctx = dot(cot, out_w[...], 1, 1).astype(BF)
        for g in range(4):
            lanes = slice(128 * g, 128 * g + 128)
            query = halves(proj[:, lanes])
            key = proj[:, 512 + 128 * g : 640 + 128 * g]
            value = proj[:, 1024 + 128 * g : 1152 + 128 * g]
            grad_out = halves(grad_ctx[:, lanes])
            attend = att[g]
            grad_att = dot(grad_out, value, 1, 1)
            total = jnp.sum(attend * grad_att, -1, keepdims=True)
            grad_scores = (attend * (grad_att - total) * 0.125).astype(BF)
            gproj[:, lanes] = merge(dot(grad_scores, key)).astype(BF)
            gproj[:, 512 + 128 * g : 640 + 128 * g] = dot(grad_scores, query, 0, 0).astype(BF)
            gproj[:, 1024 + 128 * g : 1152 + 128 * g] = dot(attend.astype(BF), grad_out, 0, 0).astype(BF)
        store_blocks(res_g, base, dot(gproj[...], qkv_w[...], 1, 1).astype(BF), 4)
        send_back(slot, res_g, ret_g, sg, rg)
        return carry

    lax.fori_loop(0, 2, window, 0)

    a_copy = pltpu.make_async_remote_copy(
        src_ref=a_src, dst_ref=a_dst, send_sem=a_sem.at[0], recv_sem=a_sem.at[1],
        device_id=(zl * 2 + 1 - core, lon), device_id_type=MESH,
    )
    a_copy.wait()
    for x_ in range(4):
        both = acc[2 * x_ : 2 * x_ + 2, core] + a_dst[2 * x_ : 2 * x_ + 2].astype(F32)
        both = both.astype(BF).reshape(64, D)
        for y_ in range(4):
            b_src[y_ * 4 + x_] = both[:, 128 * y_ : 128 * y_ + 128]

    def b_copy(d):
        partner = yx ^ d
        return pltpu.make_async_remote_copy(
            src_ref=b_src.at[partner], dst_ref=b_dst.at[yx], send_sem=bs_sem.at[partner], recv_sem=br_sem.at[yx],
            device_id=at(partner // 4, partner % 4, z, core), device_id_type=MESH,
        )

    def b_start(d, carry):
        b_copy(d).start()
        return carry

    lax.fori_loop(1, 16, b_start, 0)
    b_dst[yx] = b_src[yx]

    def b_wait(d, carry):
        partner = yx ^ d
        pltpu.make_async_copy(b_dst.at[partner], b_dst.at[partner], br_sem.at[partner]).wait()
        pltpu.make_async_copy(b_src.at[partner], b_src.at[partner], bs_sem.at[partner]).wait()
        return carry

    lax.fori_loop(1, 16, b_wait, 0)
    c_src[...] = jnp.sum(b_dst[...].astype(F32), 0).reshape(2, 32, 128)

    for t in range(4):
        z_ = (t // 2) * 8 + 2 * x + t % 2

        @pl.when(z_ != z)
        def _():
            pltpu.make_async_remote_copy(
                src_ref=c_src.at[t % 2], dst_ref=c_dst.at[z], send_sem=cs_sem.at[t], recv_sem=cr_sem.at[z],
                device_id=at(y, x, z_, core), device_id_type=MESH,
            ).start()

    @pl.when(collector)
    def _():
        c_dst[z] = c_src[zl % 2]

        def c_wait(d, carry):
            partner = z ^ d
            pltpu.make_async_copy(c_dst.at[partner], c_dst.at[partner], cr_sem.at[partner]).wait()
            return carry

        lax.fori_loop(1, 16, c_wait, 0)
        d_src[...] = jnp.sum(c_dst[...], 0)
        for d in range(1, 4):
            pltpu.make_async_remote_copy(
                src_ref=d_src, dst_ref=d_dst, send_sem=ds_sem.at[d], recv_sem=dr_sem,
                device_id=at(y, x ^ d, z, core), device_id_type=MESH,
            ).start()

    for k in range(8):
        landed(ret_b, rb, k)
        landed(ret_g, rg, k)
    from_blocks = ones_where(grid_row(iota((1, 288), 1)) == iota((384, 288), 0))
    branch = dot(from_blocks, load_blocks(ret_b, 0, 8))
    wide = pad[0].reshape(384, D).astype(F32)
    layer_ref[...] = (wide + branch).astype(BF).reshape(24, 16, D)[:, 0:12]
    grad = dot(from_blocks, load_blocks(ret_g, 0, 8))
    normed_hat = hat[...]
    centred = grad - jnp.mean(grad, -1, keepdims=True)
    back = inv[...] * (centred - normed_hat * jnp.mean(grad * normed_hat, -1, keepdims=True))
    wide = pad[1].reshape(384, D).astype(F32)
    grad_ref[...] = (wide + back).astype(BF).reshape(24, 16, D)[:, 0:12]

    @pl.when(jnp.logical_not(collector))
    def _():
        pltpu.make_async_copy(d_dst, d_dst, dr_sem).wait()

    block = jnp.where(collector, d_src[...], d_dst[...])
    dw_ref[...] = pltpu.roll(block, (128 - 16 * (h * 4 + x)) % 128, 1)[:, 0:16]

    for k, (hlat, hlon, _) in enumerate(hosts):
        sent(out_f, sf, k, hlat, hlon)
        sent(out_c, sc, k, hlat, hlon)
    for i, (slat, slon, _) in enumerate(sources):
        sent(res_b, sb, i, slat, slon)
        sent(res_g, sg, i, slat, slon)
    for t in range(4):
        z_ = (t // 2) * 8 + 2 * x + t % 2

        @pl.when(z_ != z)
        def _():
            pltpu.make_async_copy(c_src.at[t % 2], c_src.at[t % 2], cs_sem.at[t]).wait()

    @pl.when(collector)
    def _():
        for d in range(1, 4):
            pltpu.make_async_copy(d_src, d_src, ds_sem.at[d]).wait()


def on_device(fields, qkv_weight, out_weight, cotangent):
    grid_shape = fields.shape
    tokens = fields.size // D * lax.axis_size("lat") * lax.axis_size("lon")
    factor = 1.0 / math.sqrt(tokens)
    vmem = pl.BlockSpec(memory_space=pltpu.VMEM)
    hbm = pl.BlockSpec(memory_space=pl.ANY)
    dma = pltpu.SemaphoreType.DMA
    layer, grad, dw = pl.pallas_call(
        functools.partial(kernel, factor),
        out_shape=[
            jax.ShapeDtypeStruct((24, 12, D), BF),
            jax.ShapeDtypeStruct((24, 12, D), BF),
            jax.ShapeDtypeStruct((32, 16), F32),
        ],
        in_specs=[vmem, hbm, hbm, vmem],
        out_specs=[vmem, vmem, vmem],
        scratch_shapes=[
            pltpu.VMEM((2, 24, 16, D), BF),
            pltpu.VMEM((384, D), F32),
            pltpu.VMEM((384, 1), F32),
            pltpu.VMEM((D, 3 * D), BF),
            pltpu.VMEM((D, D), BF),
        ]
        + [pltpu.VMEM((8,) + BLOCK, BF)] * 8
        + [
            pltpu.VMEM((144, 3 * D), BF),
            pltpu.VMEM((4, 288, 144), F32),
            pltpu.VMEM((144, D), BF),
            pltpu.VMEM((144, 3 * D), BF),
            pltpu.VMEM((8, 2, 32, D), F32),
            pltpu.VMEM((8, 32, D), BF),
            pltpu.VMEM((8, 32, D), BF),
            pltpu.VMEM((16, 64, 128), BF),
            pltpu.VMEM((16, 64, 128), BF),
            pltpu.VMEM((2, 32, 128), F32),
            pltpu.VMEM((16, 32, 128), F32),
            pltpu.VMEM((32, 128), F32),
            pltpu.VMEM((32, 128), F32),
            dma((2,)),
        ]
        + [dma((8,))] * 8
        + [dma((2,)), dma((16,)), dma((16,)), dma((4,)), dma((16,)), dma((4,)), dma],
        compiler_params=pltpu.CompilerParams(
            collective_id=0, has_side_effects=True, vmem_limit_bytes=48 * 2**20
        ),
        cost_estimate=pl.CostEstimate(flops=1_600_000_000, bytes_accessed=4_000_000, transcendentals=400_000),
        name="window_attention",
    )(fields.reshape(24, 12, D), qkv_weight, out_weight, cotangent.reshape(24, 12, D))
    return layer.reshape(grid_shape), grad.reshape(grid_shape), dw


def solution(mesh):
    in_specs = (P(None, "lat", "lon", None), P(), P(), P(None, "lat", "lon", None))
    out_specs = (P(None, "lat", "lon", None), P(None, "lat", "lon", None), P("lat", "lon"))
    return jax.shard_map(
        on_device, mesh=mesh, in_specs=in_specs, out_specs=out_specs, check_vma=False
    )
```

time: 524 us -> 65.1 us (0.12)
  the two profiles are of different devices: /device:TPU:32 before, /device:TPU:4 now
where the time goes in v1:
time: 65.1 us; the launch traced here: 64.8 us
  Pallas kernels  57.1 us (88%)
  local copies, waits for them, and re-layouts  7.06 us (11%)
  between operations  0.66 us (1%)
    pallas_call x1, Pallas kernels, on_device(): pl.pallas_call(functools.partial(kernel, factor), out_shape=[jax.ShapeDty...  57.1 us
    unnamed x9, local copies, waits for them, and re-layouts  7.06 us

profile of v1, /device:TPU:4, one launch (start us, length us, event | category | flops | bytes accessed | tf_op | source)
XLA Modules:
  0.0 64.8 jit_solution(14039529506884697137)
XLA Ops:
  0.6 1.0 %copy.7 = bf16[4,6,12,512]{3,2,1,0:T(8,128)(2,1)S(1)} copy(bf16[4,6,12,512]{3,0,2,1:T(4,128)(2,1)} %param.4) | data formatting | bytes 589824 | tf_op args[0]
  1.7 1.0 %copy.8 = bf16[4,6,12,512]{3,2,1,0:T(8,128)(2,1)S(1)} copy(bf16[4,6,12,512]{3,0,2,1:T(4,128)(2,1)} %param.7) | data formatting | bytes 589824 | tf_op args[3]
  2.7 0.0 copy-start
  2.7 1.4 %copy-done = bf16[512,1536]{1,0:T(8,128)(2,1)S(1)} copy-done((bf16[512,1536]{1,0:T(8,128)(2,1)S(1)}, bf16[512,1536]{1,0:T(8,128)(2,1)}, u32[]{:S(2)}) %copy-start) | copy-done | bytes 1572888
  4.1 0.0 copy-start.1
  4.1 1.0 %copy-done.1 = bf16[512,512]{1,0:T(8,128)(2,1)S(1)} copy-done((bf16[512,512]{1,0:T(8,128)(2,1)S(1)}, bf16[512,512]{1,0:T(8,128)(2,1)}, u32[]{:S(2)}) %copy-start.1) | copy-done | bytes 524312
  5.2 57.1 %window_attention.1 = (bf16[24,12,512]{2,1,0:T(8,128)(2,1)S(1)}, bf16[24,12,512]{2,1,0:T(8,128)(2,1)S(1)}, f32[32,16]{1,0:T(8,128)S(1)}) custom-call(bf16[24,12,512]{2,1,0:T(8,128)(2,1)S(1)} %bitcast.6, bf16[512,1536]{1,0:T(8,128)(2,1)S(1)} %copy-done, bf16[512,512]{1,0:T(8,128)(2,1)S(1)} %copy-done.1, bf16[24,12,512]{2,1,0:T(8,128)(2,1)S(1)} %bitcast.7), custom_call_target="tpu_custom_call" | custom-call | flops 1600000000 | bytes 4000000 | tf_op jit(solution)/shard_map/window_attention/pallas_call | solution.py:444
  62.2 0.9 %copy.9 = bf16[4,6,12,512]{3,0,2,1:T(4,128)(2,1)} copy(bf16[4,6,12,512]{3,2,1,0:T(8,128)(2,1)S(1)} %bitcast.5) | data formatting | bytes 589824
  63.2 0.9 %copy.10 = bf16[4,6,12,512]{3,0,2,1:T(4,128)(2,1)} copy(bf16[4,6,12,512]{3,2,1,0:T(8,128)(2,1)S(1)} %bitcast.4) | data formatting | bytes 589824
  64.1 0.7 %copy.11 = f32[32,16]{0,1:T(8,128)} copy(f32[32,16]{1,0:T(8,128)S(1)} %get-tuple-element.11) | data formatting | bytes 4096
Async XLA Ops:
  2.7 1.4 %copy-start = (bf16[512,1536]{1,0:T(8,128)(2,1)S(1)}, bf16[512,1536]{1,0:T(8,128)(2,1)}, u32[]{:S(2)}) copy-start(bf16[512,1536]{1,0:T(8,128)(2,1)} %qkv_hbm.1) | copy-start | bytes 4718596
  4.1 1.0 %copy-start.1 = (bf16[512,512]{1,0:T(8,128)(2,1)S(1)}, bf16[512,512]{1,0:T(8,128)(2,1)}, u32[]{:S(2)}) copy-start(bf16[512,512]{1,0:T(8,128)(2,1)} %out_hbm.1) | copy-start | bytes 1572868

commit v2 on v1

--- a/solution.py
+++ b/solution.py
@@ -16,6 +16,7 @@
 D = 512
 LATS = 16
 LONS = 32
+VMEM_LIMIT = 60 * 2**20
 BLOCK = (16, 1152)
 
 
@@ -44,37 +45,54 @@
     return jnp.where(cond, qlat, lat), jnp.where(cond, qlon, lon)
 
 
+def window_host(va, vb, slot):
+    x = vb % 4
+    odd = va % 2
+    crossing = x == (3 if slot == 0 else 0)
+    inner = x == (2 if slot == 0 else 1)
+    step = 1 - 2 * slot
+    hlat, hlon = moved(va, vb, crossing, False)
+    shift = jnp.where(crossing, -step, jnp.where(inner, step, 0)) * odd
+    return hlat, hlon + shift
+
+
+def window_of(lat, lon, slot):
+    x = lon % 4
+    odd = lat % 2
+    crossing = x == (3 - odd if slot == 0 else odd)
+    inner = jnp.logical_and(x == (3 if slot == 0 else 0), odd == 1)
+    step = 1 - 2 * slot
+    vlat, vlon = moved(lat, lon, crossing, True)
+    shift = jnp.where(crossing, step, jnp.where(inner, -step, 0)) * odd
+    return vlat, vlon + shift
+
+
 def block_host(lat, lon, r, c, p):
-    kb = lon if c == 1 else (lon + LONS - 1) % LONS
-    crossing = kb % 4 == 3
+    kb = jnp.where(c == 1, lon, (lon + LONS - 1) % LONS)
+    east = (kb + 1) % LONS
     q = (1 - r) * 2 + (1 - c)
-    east = (kb + 1) % LONS
-    if p == 0 and r == 1:
-        hlat, hlon, pos = lat, kb, q
-    elif p == 0:
-        edge = lat == 0
-        hlat = jnp.where(edge, 0, lat - 1)
-        hlon = jnp.where(edge, east, kb)
-        pos = jnp.where(edge, 4 + q - 2, q)
-    elif r == 0:
-        hlat, hlon, pos = lat, east, 4 + q
+    edge = lat == (LATS - 1 if r == 1 else 0)
+    if p == 0:
+        va = lat if r == 1 else jnp.where(edge, 0, lat - 1)
+        slot1 = edge if r == 0 else None
+        pos0, pos1 = q, 4 + q - 2
     else:
-        edge = lat == LATS - 1
-        hlat = jnp.where(edge, LATS - 1, lat + 1)
-        hlon = jnp.where(edge, kb, east)
-        pos = jnp.where(edge, q + 2, 4 + q)
-    hlat, hlon = moved(hlat, hlon, crossing, False)
-    return hlat, hlon, pos
-
-
-def virtual_host(lat, lon, slot):
-    x = lon % 4
-    crossing = x == jnp.where(slot == 0, 3, 0)
-    return moved(lat, lon, crossing, True)
+        va = lat if r == 0 else jnp.where(edge, lat, lat + 1)
+        slot1 = None if r == 0 else jnp.logical_not(edge)
+        pos0, pos1 = q + 2, 4 + q
+    zero = window_host(va, kb, 0)
+    one = window_host(va, east, 1)
+    if slot1 is None:
+        (hlat, hlon), pos = (zero, pos0) if p == 0 else (one, pos1)
+    else:
+        hlat, hlon = jnp.where(slot1, one[0], zero[0]), jnp.where(slot1, one[1], zero[1])
+        pos = jnp.where(slot1, pos1, pos0)
+    relayed = jnp.logical_and(kb % 4 == 3, va % 2 == 1)
+    return hlat, hlon, pos, relayed
 
 
 def inbox_source(lat, lon, slot, q):
-    va, vb = virtual_host(lat, lon, slot)
+    va, vb = window_of(lat, lon, slot)
     south, east = q // 2, q % 2
     if slot == 0:
         edge = va == LATS - 1
@@ -106,7 +124,7 @@
     t = t - 18 * l2
     r3 = jnp.where(t >= 6, 1, 0) + jnp.where(t >= 12, 1, 0)
     lev = (1 + 2 * p + l2) & 3
-    return (lev * 6 + 3 * r + r3) * 16 + 6 * c + t - 6 * r3
+    return ((3 * r + r3) * 12 + 6 * c + t - 6 * r3) * 4 + lev
 
 
 def tail_map(count, j):
@@ -148,13 +166,13 @@
 
 def kernel(
     factor,
-    fields_ref, qkv_hbm, out_hbm, cot_ref,
+    fields_hbm, qkv_hbm, out_hbm, cot_hbm,
     layer_ref, grad_ref, dw_ref,
-    pad, hat, inv, qkv_w, out_w,
-    out_f, out_c, in_f, in_c, res_b, res_g, ret_b, ret_g,
+    raw, wide_f, wide_c, hat, inv, dw_t, qkv_w, out_w,
+    out_f, out_c, in_f, in_c, res_b, res_g, ret_b, ret_g, rel_f, rel_c,
     proj, att, ctx, gproj, acc,
     a_src, a_dst, b_src, b_dst, c_src, c_dst, d_src, d_dst,
-    w_sem, sf, sc, sb, sg, rf, rc, rb, rg,
+    w_sem, sf, sc, sb, sg, rf, rc, rb, rg, tf, tc, uf, uc,
     a_sem, bs_sem, br_sem, cs_sem, cr_sem, ds_sem, dr_sem,
 ):
     lat = lax.axis_index("lat")
@@ -171,15 +189,30 @@
     def same(dlat, dlon):
         return jnp.logical_and(dlat == lat, dlon == lon)
 
+    load_x = [
+        pltpu.make_async_copy(fields_hbm, raw.at[0], w_sem.at[0]),
+        pltpu.make_async_copy(cot_hbm, raw.at[1], w_sem.at[1]),
+    ]
     load_w = [
-        pltpu.make_async_copy(qkv_hbm, qkv_w, w_sem.at[0]),
-        pltpu.make_async_copy(out_hbm, out_w, w_sem.at[1]),
+        pltpu.make_async_copy(qkv_hbm, qkv_w, w_sem.at[2]),
+        pltpu.make_async_copy(out_hbm, out_w, w_sem.at[3]),
     ]
-    for copy in load_w:
+    for copy in load_x + load_w:
         copy.start()
 
-    hosts = [block_host(lat, lon, k >> 2, (k >> 1) & 1, k & 1) for k in range(8)]
+    far = jnp.where(x >= 2, 1, 0)
+    hosts = []
+    for j in range(8):
+        r, p, c = (j >> 1) & 1, j & 1, far if j < 4 else 1 - far
+        hosts.append(((r * 2 + c) * 2 + p,) + block_host(lat, lon, r, c, p))
     sources = [inbox_source(lat, lon, i // 4, i % 4) for i in range(8)]
+    outer = lon + 2 * far - 1
+    inner = lon + 1 - 2 * far
+    relays = jnp.logical_or(x == 1, x == 2)
+    passed = []
+    for j in range(4):
+        hlat, hlon, pos, relayed = block_host(lat, jnp.where(relays, outer, lon), (j >> 1) & 1, far, j & 1)
+        passed.append((jnp.logical_and(relays, relayed), hlat, hlon, pos))
 
     barrier = pltpu.get_barrier_semaphore()
 
@@ -187,10 +220,16 @@
         pl.semaphore_signal(barrier, inc=1, device_id=(dlat, dlon), device_id_type=MESH)
 
     due = jnp.int32(16)
-    for slat, slon, _ in sources:
+    for slat, slon, k in sources:
+        cross = (jnp.where((k & 2) != 0, slon, slon + LONS - 1) % 4) == 3
+        by = jnp.logical_and(cross, lat % 2 == 1)
+        slon = slon + jnp.where(by, jnp.where(slon % 4 == 3, -1, 1), 0)
         pl.when(jnp.logical_not(same(slat, slon)))(functools.partial(tell, slat, slon))
-    for hlat, hlon, _ in hosts:
+    for j, (_, hlat, hlon, _, relayed) in enumerate(hosts):
         due = due + jnp.where(same(hlat, hlon), 0, 1)
+    for flag, *_ in passed:
+        due = due + jnp.where(flag, 1, 0)
+        pl.when(flag)(functools.partial(tell, lat, outer))
     tell(zl * 2 + 1 - core, lon)
 
     def tell_plane(d, carry):
@@ -210,18 +249,21 @@
 
     due = due + jnp.where(collector, 3, 4)
 
-    pad[...] = jnp.zeros_like(pad)
-    pad[0, :, 0:12, :] = fields_ref[...]
-    pad[1, :, 0:12, :] = cot_ref[...]
-    wide = pad[0].reshape(384, D).astype(F32)
+    to_blocks = ones_where(grid_row(iota((288, 1), 0)) == iota((288, 288), 1))
+    load_x[0].wait()
+    for i in range(72):
+        wide_f[4 * i : 4 * i + 4] = raw[0, i].astype(F32)
+    wide = wide_f[...]
     centred = wide - jnp.mean(wide, -1, keepdims=True)
     inverse = lax.rsqrt(jnp.mean(centred * centred, -1, keepdims=True) + EPSILON)
     normed_hat = centred * inverse
     hat[...] = normed_hat
     inv[...] = inverse
-    to_blocks = ones_where(grid_row(iota((288, 1), 0)) == iota((288, 384), 1))
     store_blocks(out_f, 0, dot(to_blocks, normed_hat.astype(BF)).astype(BF), 8)
-    store_blocks(out_c, 0, dot(to_blocks, pad[1].reshape(384, D)).astype(BF), 8)
+    load_x[1].wait()
+    for i in range(72):
+        wide_c[4 * i : 4 * i + 4] = raw[1, i].astype(F32)
+    store_blocks(out_c, 0, dot(to_blocks, wide_c[...].astype(BF)).astype(BF), 8)
 
     pl.semaphore_wait(barrier, due)
 
@@ -247,9 +289,29 @@
         def _():
             pltpu.make_async_copy(src.at[i], src.at[i], sems.at[i]).wait()
 
-    for src, dst, ss, rs in ((out_f, in_f, sf, rf), (out_c, in_c, sc, rc)):
-        for k, (hlat, hlon, pos) in enumerate(hosts):
-            send(src, dst, ss, rs, k, hlat, hlon, pos)
+    def relay_copy(src, dst, send_sems, recv_sems, k, j):
+        return pltpu.make_async_remote_copy(
+            src_ref=src.at[k], dst_ref=dst.at[j], send_sem=send_sems.at[k], recv_sem=recv_sems.at[j],
+            device_id=(lat, inner), device_id_type=MESH,
+        )
+
+    halo = ((out_f, in_f, rel_f, sf, rf, tf, uf), (out_c, in_c, rel_c, sc, rc, tc, uc))
+    for src, dst, rel, ss, rs, ts, us in halo:
+        for j, (k, hlat, hlon, pos, relayed) in enumerate(hosts):
+            if j < 4:
+                pl.when(relayed)(lambda: relay_copy(src, rel, ss, ts, k, j).start())
+                pl.when(jnp.logical_not(relayed))(lambda: send(src, dst, ss, rs, k, hlat, hlon, pos))
+            else:
+                send(src, dst, ss, rs, k, hlat, hlon, pos)
+    for src, dst, rel, ss, rs, ts, us in halo:
+        for j, (flag, hlat, hlon, pos) in enumerate(passed):
+            @pl.when(flag)
+            def _():
+                landed(rel, ts, j)
+                pltpu.make_async_remote_copy(
+                    src_ref=rel.at[j], dst_ref=dst.at[pos], send_sem=us.at[j], recv_sem=rs.at[pos],
+                    device_id=(hlat, hlon), device_id_type=MESH,
+                ).start()
 
     for copy in load_w:
         copy.wait()
@@ -271,10 +333,55 @@
                     slat, slon, k = sources[s * 4 + q]
                     send(src, dst, ss, rs, s * 4 + q, slat, slon, k)
 
+    def a_copy():
+        return pltpu.make_async_remote_copy(
+            src_ref=a_src, dst_ref=a_dst, send_sem=a_sem.at[0], recv_sem=a_sem.at[1],
+            device_id=(zl * 2 + 1 - core, lon), device_id_type=MESH,
+        )
+
+    def core_to_plane():
+        a_copy().wait()
+        for x_ in range(4):
+            both = acc[2 * x_ : 2 * x_ + 2, core] + a_dst[2 * x_ : 2 * x_ + 2].astype(F32)
+            both = both.astype(BF).reshape(64, D)
+            for y_ in range(4):
+                b_src[y_ * 4 + x_] = both[:, 128 * y_ : 128 * y_ + 128]
+
+        def start(d, carry):
+            partner = yx ^ d
+            pltpu.make_async_remote_copy(
+                src_ref=b_src.at[partner], dst_ref=b_dst.at[yx], send_sem=bs_sem.at[partner], recv_sem=br_sem.at[yx],
+                device_id=at(partner // 4, partner % 4, z, core), device_id_type=MESH,
+            ).start()
+            return carry
+
+        lax.fori_loop(1, 16, start, 0)
+        b_dst[yx] = b_src[yx]
+
+    def plane_to_ring():
+        def wait(d, carry):
+            partner = yx ^ d
+            pltpu.make_async_copy(b_dst.at[partner], b_dst.at[partner], br_sem.at[partner]).wait()
+            pltpu.make_async_copy(b_src.at[partner], b_src.at[partner], bs_sem.at[partner]).wait()
+            return carry
+
+        lax.fori_loop(1, 16, wait, 0)
+        c_src[...] = jnp.sum(b_dst[...].astype(F32), 0).reshape(2, 32, 128)
+        for t in range(4):
+            z_ = (t // 2) * 8 + 2 * x + t % 2
+
+            @pl.when(z_ != z)
+            def _():
+                pltpu.make_async_remote_copy(
+                    src_ref=c_src.at[t % 2], dst_ref=c_dst.at[z], send_sem=cs_sem.at[t], recv_sem=cr_sem.at[z],
+                    device_id=at(y, x, z_, core), device_id_type=MESH,
+                ).start()
+
+    edges = [window_of(lat, lon, 0)[0] == LATS - 1, window_of(lat, lon, 1)[0] == 0]
+
     def window(i, carry):
-        slot = jnp.where(x == 0, i, 1 - i)
-        va, _ = virtual_host(lat, lon, slot)
-        edge = va == jnp.where(slot == 0, LATS - 1, 0)
+        slot = jnp.where(x == 3 - core, 1 - i, i)
+        edge = jnp.where(slot == 0, edges[0], edges[1])
         base = slot * 4
         for q in range(4):
             landed(in_f, rf, base + q)
@@ -308,13 +415,12 @@
         def _():
             acc[...] = (acc[...] + term) * factor
             a_src[...] = acc[:, 1 - core].astype(BF)
-            pltpu.make_async_remote_copy(
-                src_ref=a_src, dst_ref=a_dst, send_sem=a_sem.at[0], recv_sem=a_sem.at[1],
-                device_id=(zl * 2 + 1 - core, lon), device_id_type=MESH,
-            ).start()
+            a_copy().start()
 
         grad_ctx = dot(cot, out_w[...], 1, 1).astype(BF)
         for g in range(4):
+            if g == 2:
+                pl.when(i == 1)(core_to_plane)
             lanes = slice(128 * g, 128 * g + 128)
             query = halves(proj[:, lanes])
             key = proj[:, 512 + 128 * g : 640 + 128 * g]
@@ -329,53 +435,10 @@
             gproj[:, 1024 + 128 * g : 1152 + 128 * g] = dot(attend.astype(BF), grad_out, 0, 0).astype(BF)
         store_blocks(res_g, base, dot(gproj[...], qkv_w[...], 1, 1).astype(BF), 4)
         send_back(slot, res_g, ret_g, sg, rg)
+        pl.when(i == 1)(plane_to_ring)
         return carry
 
     lax.fori_loop(0, 2, window, 0)
-
-    a_copy = pltpu.make_async_remote_copy(
-        src_ref=a_src, dst_ref=a_dst, send_sem=a_sem.at[0], recv_sem=a_sem.at[1],
-        device_id=(zl * 2 + 1 - core, lon), device_id_type=MESH,
-    )
-    a_copy.wait()
-    for x_ in range(4):
-        both = acc[2 * x_ : 2 * x_ + 2, core] + a_dst[2 * x_ : 2 * x_ + 2].astype(F32)
-        both = both.astype(BF).reshape(64, D)
-        for y_ in range(4):
-            b_src[y_ * 4 + x_] = both[:, 128 * y_ : 128 * y_ + 128]
-
-    def b_copy(d):
-        partner = yx ^ d
-        return pltpu.make_async_remote_copy(
-            src_ref=b_src.at[partner], dst_ref=b_dst.at[yx], send_sem=bs_sem.at[partner], recv_sem=br_sem.at[yx],
-            device_id=at(partner // 4, partner % 4, z, core), device_id_type=MESH,
-        )
-
-    def b_start(d, carry):
-        b_copy(d).start()
-        return carry
-
-    lax.fori_loop(1, 16, b_start, 0)
-    b_dst[yx] = b_src[yx]
-
-    def b_wait(d, carry):
-        partner = yx ^ d
-        pltpu.make_async_copy(b_dst.at[partner], b_dst.at[partner], br_sem.at[partner]).wait()
-        pltpu.make_async_copy(b_src.at[partner], b_src.at[partner], bs_sem.at[partner]).wait()
-        return carry
-
-    lax.fori_loop(1, 16, b_wait, 0)
-    c_src[...] = jnp.sum(b_dst[...].astype(F32), 0).reshape(2, 32, 128)
-
-    for t in range(4):
-        z_ = (t // 2) * 8 + 2 * x + t % 2
-
-        @pl.when(z_ != z)
-        def _():
-            pltpu.make_async_remote_copy(
-                src_ref=c_src.at[t % 2], dst_ref=c_dst.at[z], send_sem=cs_sem.at[t], recv_sem=cr_sem.at[z],
-                device_id=at(y, x, z_, core), device_id_type=MESH,
-            ).start()
 
     @pl.when(collector)
     def _():
@@ -396,28 +459,31 @@
 
     for k in range(8):
         landed(ret_b, rb, k)
+    from_blocks = ones_where(grid_row(iota((1, 288), 1)) == iota((288, 288), 0))
+    wide_f[...] += dot(from_blocks, load_blocks(ret_b, 0, 8))
+    for i in range(72):
+        layer_ref[i] = wide_f[4 * i : 4 * i + 4].astype(BF)
+    for k in range(8):
         landed(ret_g, rg, k)
-    from_blocks = ones_where(grid_row(iota((1, 288), 1)) == iota((384, 288), 0))
-    branch = dot(from_blocks, load_blocks(ret_b, 0, 8))
-    wide = pad[0].reshape(384, D).astype(F32)
-    layer_ref[...] = (wide + branch).astype(BF).reshape(24, 16, D)[:, 0:12]
     grad = dot(from_blocks, load_blocks(ret_g, 0, 8))
     normed_hat = hat[...]
     centred = grad - jnp.mean(grad, -1, keepdims=True)
-    back = inv[...] * (centred - normed_hat * jnp.mean(grad * normed_hat, -1, keepdims=True))
-    wide = pad[1].reshape(384, D).astype(F32)
-    grad_ref[...] = (wide + back).astype(BF).reshape(24, 16, D)[:, 0:12]
+    wide_c[...] += inv[...] * (centred - normed_hat * jnp.mean(grad * normed_hat, -1, keepdims=True))
+    for i in range(72):
+        grad_ref[i] = wide_c[4 * i : 4 * i + 4].astype(BF)
 
     @pl.when(jnp.logical_not(collector))
     def _():
         pltpu.make_async_copy(d_dst, d_dst, dr_sem).wait()
 
-    block = jnp.where(collector, d_src[...], d_dst[...])
-    dw_ref[...] = pltpu.roll(block, (128 - 16 * (h * 4 + x)) % 128, 1)[:, 0:16]
-
-    for k, (hlat, hlon, _) in enumerate(hosts):
-        sent(out_f, sf, k, hlat, hlon)
-        sent(out_c, sc, k, hlat, hlon)
+    dw_t[...] = jnp.where(collector, d_src[...], d_dst[...]).T
+    dw_ref[...] = dw_t[pl.ds(pl.multiple_of(16 * (h * 4 + x), 16), 16)]
+
+    for src, dst, rel, ss, rs, ts, us in halo:
+        for k, hlat, hlon, _, _ in hosts:
+            sent(src, ss, k, hlat, hlon)
+        for j, (flag, *_) in enumerate(passed):
+            pl.when(flag)(lambda: pltpu.make_async_copy(rel.at[j], rel.at[j], us.at[j]).wait())
     for i, (slat, slon, _) in enumerate(sources):
         sent(res_b, sb, i, slat, slon)
         sent(res_g, sg, i, slat, slon)
@@ -439,25 +505,29 @@
     tokens = fields.size // D * lax.axis_size("lat") * lax.axis_size("lon")
     factor = 1.0 / math.sqrt(tokens)
     vmem = pl.BlockSpec(memory_space=pltpu.VMEM)
-    hbm = pl.BlockSpec(memory_space=pl.ANY)
+    hbm = pl.BlockSpec(memory_space=pltpu.HBM)
     dma = pltpu.SemaphoreType.DMA
     layer, grad, dw = pl.pallas_call(
         functools.partial(kernel, factor),
         out_shape=[
-            jax.ShapeDtypeStruct((24, 12, D), BF),
-            jax.ShapeDtypeStruct((24, 12, D), BF),
-            jax.ShapeDtypeStruct((32, 16), F32),
+            jax.ShapeDtypeStruct((72, 4, D), BF),
+            jax.ShapeDtypeStruct((72, 4, D), BF),
+            jax.ShapeDtypeStruct((16, 32), F32),
         ],
-        in_specs=[vmem, hbm, hbm, vmem],
+        in_specs=[hbm, hbm, hbm, hbm],
         out_specs=[vmem, vmem, vmem],
         scratch_shapes=[
-            pltpu.VMEM((2, 24, 16, D), BF),
-            pltpu.VMEM((384, D), F32),
-            pltpu.VMEM((384, 1), F32),
+            pltpu.VMEM((2, 72, 4, D), BF),
+            pltpu.VMEM((288, D), F32),
+            pltpu.VMEM((288, D), F32),
+            pltpu.VMEM((288, D), F32),
+            pltpu.VMEM((288, 1), F32),
+            pltpu.VMEM((128, 32), F32),
             pltpu.VMEM((D, 3 * D), BF),
             pltpu.VMEM((D, D), BF),
         ]
         + [pltpu.VMEM((8,) + BLOCK, BF)] * 8
+        + [pltpu.VMEM((4,) + BLOCK, BF)] * 2
         + [
             pltpu.VMEM((144, 3 * D), BF),
             pltpu.VMEM((4, 288, 144), F32),
@@ -472,17 +542,44 @@
             pltpu.VMEM((16, 32, 128), F32),
             pltpu.VMEM((32, 128), F32),
             pltpu.VMEM((32, 128), F32),
-            dma((2,)),
+            dma((4,)),
         ]
         + [dma((8,))] * 8
+        + [dma((4,))] * 4
         + [dma((2,)), dma((16,)), dma((16,)), dma((4,)), dma((16,)), dma((4,)), dma],
         compiler_params=pltpu.CompilerParams(
-            collective_id=0, has_side_effects=True, vmem_limit_bytes=48 * 2**20
+            collective_id=0, has_side_effects=True, vmem_limit_bytes=VMEM_LIMIT
         ),
         cost_estimate=pl.CostEstimate(flops=1_600_000_000, bytes_accessed=4_000_000, transcendentals=400_000),
         name="window_attention",
-    )(fields.reshape(24, 12, D), qkv_weight, out_weight, cotangent.reshape(24, 12, D))
-    return layer.reshape(grid_shape), grad.reshape(grid_shape), dw
+    )(by_place(fields), qkv_weight, out_weight, by_place(cotangent))
+    layer, grad, dw = hand_out(layer, grad, dw)
+    return from_place(layer, grid_shape), from_place(grad, grid_shape), dw.T
+
+
+def hand_out(*arrays):
+    count = len(arrays)
+
+    def kernel(*refs):
+        for i in range(count):
+            refs[count + i][...] = refs[i][...]
+
+    return pl.pallas_call(
+        kernel,
+        out_shape=[jax.ShapeDtypeStruct(a.shape, a.dtype) for a in arrays],
+        in_specs=[pl.BlockSpec(memory_space=pltpu.VMEM)] * count,
+        out_specs=[pl.BlockSpec(memory_space=pltpu.VMEM)] * count,
+        name="hand_out",
+    )(*arrays)
+
+
+def by_place(grid):
+    return grid.transpose(1, 2, 0, 3).reshape(72, 4, D)
+
+
+def from_place(tokens, grid_shape):
+    lev, lat, lon, d = grid_shape
+    return tokens.reshape(lat, lon, lev, d).transpose(2, 0, 1, 3)
 
 
 def solution(mesh):

time: 65.1 us -> 56.3 us (0.86)
  local copies, waits for them, and re-layouts: 7.06 us -> 0 us
  Pallas kernels: 57.1 us -> 55.5 us
    unnamed x9 -> x0, local copies, waits for them, and re-layouts: 7.06 us -> none
    pallas_call x1, Pallas kernels: 57.1 us -> 53.6 us  [on_device(): pl.pallas_call(functools.partial(kernel, factor), out_shape=[jax.ShapeDty...]
    pallas_call x0 -> x1, Pallas kernels: none -> 1.89 us  [hand_out(): pl.pallas_call(kernel, out_shape=[jax.ShapeDtypeStruct(a.shape, a.dtype)...]
where the time goes in v2:
time: 56.3 us; the launch traced here: 56.2 us
  Pallas kernels  55.5 us (99%)
  between operations  0.64 us (1%)
    pallas_call x1, Pallas kernels, on_device(): pl.pallas_call(functools.partial(kernel, factor), out_shape=[jax.ShapeDty...  53.6 us
    pallas_call x1, Pallas kernels, hand_out(): pl.pallas_call(kernel, out_shape=[jax.ShapeDtypeStruct(a.shape, a.dtype)...  1.89 us

profile of v2, /device:TPU:4, one launch (start us, length us, event | category | flops | bytes accessed | tf_op | source)
XLA Modules:
  0.0 56.2 jit_solution(10642793946909333904)
XLA Ops:
  0.6 53.6 %window_attention.1 = (bf16[72,4,512]{2,1,0:T(4,128)(2,1)}, bf16[72,4,512]{2,1,0:T(4,128)(2,1)}, f32[16,32]{1,0:T(8,128)}) custom-call(bf16[72,4,512]{2,1,0:T(4,128)(2,1)} %bitcast.13, bf16[512,1536]{1,0:T(8,128)(2,1)} %qkv_hbm.1, bf16[512,512]{1,0:T(8,128)(2,1)} %out_hbm.1, bf16[72,4,512]{2,1,0:T(4,128)(2,1)} %bitcast.14), custom_call_target="tpu_custom_call" | custom-call | flops 1600000000 | bytes 4000000 | tf_op jit(solution)/shard_map/window_attention/pallas_call | solution.py:510
  54.3 1.9 %hand_out.1 = (bf16[72,4,512]{2,1,0:T(4,128)(2,1)}, bf16[72,4,512]{2,1,0:T(4,128)(2,1)}, f32[16,32]{1,0:T(8,128)}) custom-call(bf16[72,4,512]{2,1,0:T(4,128)(2,1)} %get-tuple-element.9.refs_0_, bf16[72,4,512]{2,1,0:T(4,128)(2,1)} %get-tuple-element.10.refs_1_, f32[16,32]{1,0:T(8,128)} %get-tuple-element.11.refs_2_), custom_call_target="tpu_custom_call" | custom-call | tf_op jit(solution)/shard_map/hand_out/pallas_call | solution.py:567

commit v3 on v2

--- a/solution.py
+++ b/solution.py
@@ -170,10 +170,10 @@
     layer_ref, grad_ref, dw_ref,
     raw, wide_f, wide_c, hat, inv, dw_t, qkv_w, out_w,
     out_f, out_c, in_f, in_c, res_b, res_g, ret_b, ret_g, rel_f, rel_c,
-    proj, att, ctx, gproj, acc,
+    proj, att, ctx, cots, gctx, gproj, acc,
     a_src, a_dst, b_src, b_dst, c_src, c_dst, d_src, d_dst,
     w_sem, sf, sc, sb, sg, rf, rc, rb, rg, tf, tc, uf, uc,
-    a_sem, bs_sem, br_sem, cs_sem, cr_sem, ds_sem, dr_sem,
+    a_sem, bs_sem, br_sem, cs_sem, cr_sem, ds_sem, dr_sem, ring_sem,
 ):
     lat = lax.axis_index("lat")
     lon = lax.axis_index("lon")
@@ -230,7 +230,17 @@
     for flag, *_ in passed:
         due = due + jnp.where(flag, 1, 0)
         pl.when(flag)(functools.partial(tell, lat, outer))
-    tell(zl * 2 + 1 - core, lon)
+    for d in (4, 12):
+        tell(*at(y, x, (z + d) % 16, core))
+
+    @pl.when(collector)
+    def _():
+        for d in (3, 13, 2, 14, 1, 15):
+            tell(*at(y, x, (z + d) % 16, core))
+
+    for collecting in (0, 1, 8, 9):
+        away = (2 * x + collecting - z + 16) % 16
+        due = due + jnp.where((away >= 1) & (away <= 3) | (away >= 13), 1, 0)
 
     def tell_plane(d, carry):
         partner = yx ^ d
@@ -238,16 +248,9 @@
         return carry
 
     lax.fori_loop(1, 16, tell_plane, 0)
-
-    @pl.when(collector)
-    def _():
-        def tell_ring(d, carry):
-            tell(*at(y, x, z ^ d, core))
-            return carry
-
-        lax.fori_loop(1, 16, tell_ring, 0)
-
-    due = due + jnp.where(collector, 3, 4)
+    tell(zl * 2 + 1 - core, lon)
+
+    due = due + 2
 
     to_blocks = ones_where(grid_row(iota((288, 1), 0)) == iota((288, 288), 1))
     load_x[0].wait()
@@ -266,6 +269,10 @@
     store_blocks(out_c, 0, dot(to_blocks, wide_c[...].astype(BF)).astype(BF), 8)
 
     pl.semaphore_wait(barrier, due)
+    for d in (4, 12):
+        pl.semaphore_signal(
+            ring_sem, inc=1, device_id=at(y, x, (z + d) % 16, core), device_id_type=MESH
+        )
 
     def send(src, dst, send_sems, recv_sems, i, dlat, dlon, j):
         here = same(dlat, dlon)
@@ -297,12 +304,12 @@
 
     halo = ((out_f, in_f, rel_f, sf, rf, tf, uf), (out_c, in_c, rel_c, sc, rc, tc, uc))
     for src, dst, rel, ss, rs, ts, us in halo:
-        for j, (k, hlat, hlon, pos, relayed) in enumerate(hosts):
-            if j < 4:
-                pl.when(relayed)(lambda: relay_copy(src, rel, ss, ts, k, j).start())
-                pl.when(jnp.logical_not(relayed))(lambda: send(src, dst, ss, rs, k, hlat, hlon, pos))
-            else:
-                send(src, dst, ss, rs, k, hlat, hlon, pos)
+        for j, (k, hlat, hlon, pos, relayed) in enumerate(hosts[:4]):
+            pl.when(relayed)(lambda: relay_copy(src, rel, ss, ts, k, j).start())
+            pl.when(jnp.logical_not(relayed))(lambda: send(src, dst, ss, rs, k, hlat, hlon, pos))
+    for src, dst, rel, ss, rs, ts, us in halo:
+        for k, hlat, hlon, pos, _ in hosts[4:]:
+            send(src, dst, ss, rs, k, hlat, hlon, pos)
     for src, dst, rel, ss, rs, ts, us in halo:
         for j, (flag, hlat, hlon, pos) in enumerate(passed):
             @pl.when(flag)
@@ -326,12 +333,16 @@
         return jnp.where(first_half, stacked[:144], stacked[144:])
 
     def send_back(slot, src, dst, ss, rs):
-        for s in range(2):
-            @pl.when(slot == s)
-            def _():
-                for q in range(4):
-                    slat, slon, k = sources[s * 4 + q]
-                    send(src, dst, ss, rs, s * 4 + q, slat, slon, k)
+        def go(s):
+            for q in range(4):
+                slat, slon, k = sources[s * 4 + q]
+                send(src, dst, ss, rs, s * 4 + q, slat, slon, k)
+
+        if isinstance(slot, int):
+            go(slot)
+        else:
+            for s in range(2):
+                pl.when(slot == s)(functools.partial(go, s))
 
     def a_copy():
         return pltpu.make_async_remote_copy(
@@ -366,7 +377,8 @@
             return carry
 
         lax.fori_loop(1, 16, wait, 0)
-        c_src[...] = jnp.sum(b_dst[...].astype(F32), 0).reshape(2, 32, 128)
+        c_src[...] = jnp.sum(b_dst[...].astype(F32), 0).astype(BF).reshape(2, 32, 128)
+        pl.semaphore_wait(ring_sem, 2)
         for t in range(4):
             z_ = (t // 2) * 8 + 2 * x + t % 2
 
@@ -379,66 +391,70 @@
 
     edges = [window_of(lat, lon, 0)[0] == LATS - 1, window_of(lat, lon, 1)[0] == 0]
 
-    def window(i, carry):
-        slot = jnp.where(x == 3 - core, 1 - i, i)
+    def slot_of(i):
+        return jnp.where(x == 3 - core, 1 - i, i)
+
+    def forward(i, carry):
+        slot = slot_of(i)
         edge = jnp.where(slot == 0, edges[0], edges[1])
-        base = slot * 4
         for q in range(4):
-            landed(in_f, rf, base + q)
-        tokens = load_blocks(in_f, base, 4)
-        proj[...] = dot(tokens, qkv_w[...]).astype(BF)
+            landed(in_f, rf, slot * 4 + q)
+        proj[slot] = dot(load_blocks(in_f, slot * 4, 4), qkv_w[...]).astype(BF)
         allowed = group_ids(iota((144, 1), 0), slot, edge) == group_ids(iota((1, 144), 1), slot, edge)
         allowed = jnp.concatenate([allowed, allowed], 0)
         for g in range(4):
             lanes = slice(128 * g, 128 * g + 128)
-            query = halves(proj[:, lanes])
-            key = proj[:, 512 + 128 * g : 640 + 128 * g]
-            value = proj[:, 1024 + 128 * g : 1152 + 128 * g]
+            query = halves(proj[slot, :, lanes])
+            key = proj[slot, :, 512 + 128 * g : 640 + 128 * g]
+            value = proj[slot, :, 1024 + 128 * g : 1152 + 128 * g]
             scores = jnp.where(allowed, dot(query, key, 1, 1) * 0.125, MASK_FILL)
             lifted = jnp.exp(scores - jnp.max(scores, -1, keepdims=True))
             attend = lifted * (1.0 / jnp.sum(lifted, -1, keepdims=True))
-            att[g] = attend
-            ctx[:, lanes] = merge(dot(attend.astype(BF), value)).astype(BF)
-        store_blocks(res_b, base, dot(ctx[...], out_w[...]).astype(BF), 4)
+            att[slot * 4 + g] = attend
+            ctx[slot, :, lanes] = merge(dot(attend.astype(BF), value)).astype(BF)
+        return carry
+
+    lax.fori_loop(0, 2, forward, 0)
+
+    for i in range(2):
+        slot = slot_of(i)
+        for q in range(4):
+            landed(in_c, rc, slot * 4 + q)
+        cots[slot] = load_blocks(in_c, slot * 4, 4)
+    both_ctx = ctx[...].reshape(288, D)
+    both_cot = cots[...].reshape(288, D)
+    acc[...] = (dot(both_ctx, both_cot, 0, 0) * factor).reshape(8, 2, 32, D)
+    a_src[...] = acc[:, 1 - core].astype(BF)
+    a_copy().start()
+
+    branch = dot(both_ctx, out_w[...]).astype(BF)
+    for slot in range(2):
+        store_blocks(res_b, slot * 4, branch[144 * slot : 144 * slot + 144], 4)
         send_back(slot, res_b, ret_b, sb, rb)
-
-        for q in range(4):
-            landed(in_c, rc, base + q)
-        cot = load_blocks(in_c, base, 4)
-        term = dot(ctx[...], cot, 0, 0).reshape(8, 2, 32, D)
-
-        @pl.when(i == 0)
-        def _():
-            acc[...] = term
-
-        @pl.when(i == 1)
-        def _():
-            acc[...] = (acc[...] + term) * factor
-            a_src[...] = acc[:, 1 - core].astype(BF)
-            a_copy().start()
-
-        grad_ctx = dot(cot, out_w[...], 1, 1).astype(BF)
+    gctx[...] = dot(both_cot, out_w[...], 1, 1).astype(BF).reshape(2, 144, D)
+    core_to_plane()
+
+    def backward(i, carry):
+        slot = slot_of(i)
         for g in range(4):
-            if g == 2:
-                pl.when(i == 1)(core_to_plane)
             lanes = slice(128 * g, 128 * g + 128)
-            query = halves(proj[:, lanes])
-            key = proj[:, 512 + 128 * g : 640 + 128 * g]
-            value = proj[:, 1024 + 128 * g : 1152 + 128 * g]
-            grad_out = halves(grad_ctx[:, lanes])
-            attend = att[g]
+            query = halves(proj[slot, :, lanes])
+            key = proj[slot, :, 512 + 128 * g : 640 + 128 * g]
+            value = proj[slot, :, 1024 + 128 * g : 1152 + 128 * g]
+            grad_out = halves(gctx[slot, :, lanes])
+            attend = att[slot * 4 + g]
             grad_att = dot(grad_out, value, 1, 1)
             total = jnp.sum(attend * grad_att, -1, keepdims=True)
             grad_scores = (attend * (grad_att - total) * 0.125).astype(BF)
             gproj[:, lanes] = merge(dot(grad_scores, key)).astype(BF)
             gproj[:, 512 + 128 * g : 640 + 128 * g] = dot(grad_scores, query, 0, 0).astype(BF)
             gproj[:, 1024 + 128 * g : 1152 + 128 * g] = dot(attend.astype(BF), grad_out, 0, 0).astype(BF)
-        store_blocks(res_g, base, dot(gproj[...], qkv_w[...], 1, 1).astype(BF), 4)
+        store_blocks(res_g, slot * 4, dot(gproj[...], qkv_w[...], 1, 1).astype(BF), 4)
         send_back(slot, res_g, ret_g, sg, rg)
-        pl.when(i == 1)(plane_to_ring)
         return carry
 
-    lax.fori_loop(0, 2, window, 0)
+    lax.fori_loop(0, 2, backward, 0)
+    plane_to_ring()
 
     @pl.when(collector)
     def _():
@@ -450,7 +466,7 @@
             return carry
 
         lax.fori_loop(1, 16, c_wait, 0)
-        d_src[...] = jnp.sum(c_dst[...], 0)
+        d_src[...] = jnp.sum(c_dst[...].astype(F32), 0)
         for d in range(1, 4):
             pltpu.make_async_remote_copy(
                 src_ref=d_src, dst_ref=d_dst, send_sem=ds_sem.at[d], recv_sem=dr_sem,
@@ -529,24 +545,26 @@
         + [pltpu.VMEM((8,) + BLOCK, BF)] * 8
         + [pltpu.VMEM((4,) + BLOCK, BF)] * 2
         + [
-            pltpu.VMEM((144, 3 * D), BF),
-            pltpu.VMEM((4, 288, 144), F32),
-            pltpu.VMEM((144, D), BF),
+            pltpu.VMEM((2, 144, 3 * D), BF),
+            pltpu.VMEM((8, 288, 144), F32),
+            pltpu.VMEM((2, 144, D), BF),
+            pltpu.VMEM((2, 144, D), BF),
+            pltpu.VMEM((2, 144, D), BF),
             pltpu.VMEM((144, 3 * D), BF),
             pltpu.VMEM((8, 2, 32, D), F32),
             pltpu.VMEM((8, 32, D), BF),
             pltpu.VMEM((8, 32, D), BF),
             pltpu.VMEM((16, 64, 128), BF),
             pltpu.VMEM((16, 64, 128), BF),
-            pltpu.VMEM((2, 32, 128), F32),
-            pltpu.VMEM((16, 32, 128), F32),
+            pltpu.VMEM((2, 32, 128), BF),
+            pltpu.VMEM((16, 32, 128), BF),
             pltpu.VMEM((32, 128), F32),
             pltpu.VMEM((32, 128), F32),
             dma((4,)),
         ]
         + [dma((8,))] * 8
         + [dma((4,))] * 4
-        + [dma((2,)), dma((16,)), dma((16,)), dma((4,)), dma((16,)), dma((4,)), dma],
+        + [dma((2,)), dma((16,)), dma((16,)), dma((4,)), dma((16,)), dma((4,)), dma, pltpu.SemaphoreType.REGULAR],
         compiler_params=pltpu.CompilerParams(
             collective_id=0, has_side_effects=True, vmem_limit_bytes=VMEM_LIMIT
         ),

time: 56.3 us -> 54.3 us (0.964)
  Pallas kernels: 55.5 us -> 53.5 us
    pallas_call x1, Pallas kernels: 53.6 us -> 51.6 us  [on_device(): pl.pallas_call(functools.partial(kernel, factor), out_shape=[jax.ShapeDty...]
where the time goes in v3:
time: 54.3 us; the launch traced here: 54.1 us
  Pallas kernels  53.5 us (99%)
  between operations  0.64 us (1%)
    pallas_call x1, Pallas kernels, on_device(): pl.pallas_call(functools.partial(kernel, factor), out_shape=[jax.ShapeDty...  51.6 us
    pallas_call x1, Pallas kernels, hand_out(): pl.pallas_call(kernel, out_shape=[jax.ShapeDtypeStruct(a.shape, a.dtype)...  1.89 us

profile of v3, /device:TPU:4, one launch (start us, length us, event | category | flops | bytes accessed | tf_op | source)
XLA Modules:
  0.0 54.1 jit_solution(10599868615919614859)
XLA Ops:
  0.6 51.6 %window_attention.1 = (bf16[72,4,512]{2,1,0:T(4,128)(2,1)}, bf16[72,4,512]{2,1,0:T(4,128)(2,1)}, f32[16,32]{1,0:T(8,128)}) custom-call(bf16[72,4,512]{2,1,0:T(4,128)(2,1)} %bitcast.13, bf16[512,1536]{1,0:T(8,128)(2,1)} %qkv_hbm.1, bf16[512,512]{1,0:T(8,128)(2,1)} %out_hbm.1, bf16[72,4,512]{2,1,0:T(4,128)(2,1)} %bitcast.14), custom_call_target="tpu_custom_call" | custom-call | flops 1600000000 | bytes 4000000 | tf_op jit(solution)/shard_map/window_attention/pallas_call | solution.py:526
  52.2 1.9 %hand_out.1 = (bf16[72,4,512]{2,1,0:T(4,128)(2,1)}, bf16[72,4,512]{2,1,0:T(4,128)(2,1)}, f32[16,32]{1,0:T(8,128)}) custom-call(bf16[72,4,512]{2,1,0:T(4,128)(2,1)} %get-tuple-element.9.refs_0_, bf16[72,4,512]{2,1,0:T(4,128)(2,1)} %get-tuple-element.10.refs_1_, f32[16,32]{1,0:T(8,128)} %get-tuple-element.11.refs_2_), custom_call_target="tpu_custom_call" | custom-call | tf_op jit(solution)/shard_map/hand_out/pallas_call | solution.py:585

commit v4 on v3

--- a/solution.py
+++ b/solution.py
@@ -18,6 +18,7 @@
 LONS = 32
 VMEM_LIMIT = 60 * 2**20
 BLOCK = (16, 1152)
+FAR_FIRST = (10, 9, 11, 6, 14, 8, 2, 5, 7, 13, 15, 4, 12, 1, 3)
 
 
 def dot(a, b, ca=1, cb=0):
@@ -358,22 +359,18 @@
             for y_ in range(4):
                 b_src[y_ * 4 + x_] = both[:, 128 * y_ : 128 * y_ + 128]
 
-        def start(d, carry):
+        for d in FAR_FIRST:
             partner = yx ^ d
             pltpu.make_async_remote_copy(
                 src_ref=b_src.at[partner], dst_ref=b_dst.at[yx], send_sem=bs_sem.at[partner], recv_sem=br_sem.at[yx],
                 device_id=at(partner // 4, partner % 4, z, core), device_id_type=MESH,
             ).start()
-            return carry
-
-        lax.fori_loop(1, 16, start, 0)
         b_dst[yx] = b_src[yx]
 
     def plane_to_ring():
         def wait(d, carry):
             partner = yx ^ d
             pltpu.make_async_copy(b_dst.at[partner], b_dst.at[partner], br_sem.at[partner]).wait()
-            pltpu.make_async_copy(b_src.at[partner], b_src.at[partner], bs_sem.at[partner]).wait()
             return carry
 
         lax.fori_loop(1, 16, wait, 0)
@@ -427,12 +424,12 @@
     a_src[...] = acc[:, 1 - core].astype(BF)
     a_copy().start()
 
-    branch = dot(both_ctx, out_w[...]).astype(BF)
+    gctx[...] = dot(both_cot, out_w[...], 1, 1).astype(BF).reshape(2, 144, D)
+    core_to_plane()
+    branch = dot(ctx[...].reshape(288, D), out_w[...]).astype(BF)
     for slot in range(2):
         store_blocks(res_b, slot * 4, branch[144 * slot : 144 * slot + 144], 4)
         send_back(slot, res_b, ret_b, sb, rb)
-    gctx[...] = dot(both_cot, out_w[...], 1, 1).astype(BF).reshape(2, 144, D)
-    core_to_plane()
 
     def backward(i, carry):
         slot = slot_of(i)
@@ -495,6 +492,12 @@
     dw_t[...] = jnp.where(collector, d_src[...], d_dst[...]).T
     dw_ref[...] = dw_t[pl.ds(pl.multiple_of(16 * (h * 4 + x), 16), 16)]
 
+    def b_sent(d, carry):
+        partner = yx ^ d
+        pltpu.make_async_copy(b_src.at[partner], b_src.at[partner], bs_sem.at[partner]).wait()
+        return carry
+
+    lax.fori_loop(1, 16, b_sent, 0)
     for src, dst, rel, ss, rs, ts, us in halo:
         for k, hlat, hlon, _, _ in hosts:
             sent(src, ss, k, hlat, hlon)
@@ -526,9 +529,9 @@
     layer, grad, dw = pl.pallas_call(
         functools.partial(kernel, factor),
         out_shape=[
-            jax.ShapeDtypeStruct((72, 4, D), BF),
-            jax.ShapeDtypeStruct((72, 4, D), BF),
-            jax.ShapeDtypeStruct((16, 32), F32),
+            pltpu.VMEM((72, 4, D), BF),
+            pltpu.VMEM((72, 4, D), BF),
+            pltpu.VMEM((16, 32), F32),
         ],
         in_specs=[hbm, hbm, hbm, hbm],
         out_specs=[vmem, vmem, vmem],
@@ -571,24 +574,7 @@
         cost_estimate=pl.CostEstimate(flops=1_600_000_000, bytes_accessed=4_000_000, transcendentals=400_000),
         name="window_attention",
     )(by_place(fields), qkv_weight, out_weight, by_place(cotangent))
-    layer, grad, dw = hand_out(layer, grad, dw)
     return from_place(layer, grid_shape), from_place(grad, grid_shape), dw.T
-
-
-def hand_out(*arrays):
-    count = len(arrays)
-
-    def kernel(*refs):
-        for i in range(count):
-            refs[count + i][...] = refs[i][...]
-
-    return pl.pallas_call(
-        kernel,
-        out_shape=[jax.ShapeDtypeStruct(a.shape, a.dtype) for a in arrays],
-        in_specs=[pl.BlockSpec(memory_space=pltpu.VMEM)] * count,
-        out_specs=[pl.BlockSpec(memory_space=pltpu.VMEM)] * count,
-        name="hand_out",
-    )(*arrays)
 
 
 def by_place(grid):

time: 54.3 us -> 52.7 us (0.971)
  the two profiles are of different devices: /device:TPU:4 before, /device:TPU:1 now
where the time goes in v4:
time: 52.7 us; the launch traced here: 52.6 us
  Pallas kernels  49.9 us (95%)
  local copies, waits for them, and re-layouts  2.03 us (4%)
  between operations  0.64 us (1%)
    pallas_call x1, Pallas kernels, on_device(): pl.pallas_call(functools.partial(kernel, factor), out_shape=[pltpu.VMEM((...  49.9 us
    unnamed x3, local copies, waits for them, and re-layouts  2.03 us

profile of v4, /device:TPU:1, one launch (start us, length us, event | category | flops | bytes accessed | tf_op | source)
XLA Modules:
  0.0 52.6 jit_solution(5758961167674209294)
XLA Ops:
  0.6 49.9 %window_attention.1 = (bf16[72,4,512]{2,1,0:T(4,128)(2,1)S(1)}, bf16[72,4,512]{2,1,0:T(4,128)(2,1)S(1)}, f32[16,32]{1,0:T(8,128)S(1)}) custom-call(bf16[72,4,512]{2,1,0:T(4,128)(2,1)} %bitcast.16, bf16[512,1536]{1,0:T(8,128)(2,1)} %qkv_hbm.1, bf16[512,512]{1,0:T(8,128)(2,1)} %out_hbm.1, bf16[72,4,512]{2,1,0:T(4,128)(2,1)} %bitcast.17), custom_call_target="tpu_custom_call" | custom-call | flops 1600000000 | bytes 4000000 | tf_op jit(solution)/shard_map/window_attention/pallas_call | solution.py:529
  50.6 0.7 %copy.10 = bf16[4,6,12,512]{3,0,2,1:T(4,128)(2,1)} copy(bf16[4,6,12,512]{3,0,2,1:T(4,128)(2,1)S(1)} %bitcast.14) | data formatting | bytes 589824
  51.3 0.7 %copy.11 = bf16[4,6,12,512]{3,0,2,1:T(4,128)(2,1)} copy(bf16[4,6,12,512]{3,0,2,1:T(4,128)(2,1)S(1)} %bitcast.13) | data formatting | bytes 589824
  52.0 0.6 %copy.12 = f32[32,16]{0,1:T(8,128)} copy(f32[32,16]{0,1:T(8,128)S(1)} %bitcast.15) | data formatting | bytes 4096

commit v5 on v4

--- a/solution.py
+++ b/solution.py
@@ -18,7 +18,6 @@
 LONS = 32
 VMEM_LIMIT = 60 * 2**20
 BLOCK = (16, 1152)
-FAR_FIRST = (10, 9, 11, 6, 14, 8, 2, 5, 7, 13, 15, 4, 12, 1, 3)
 
 
 def dot(a, b, ca=1, cb=0):
@@ -201,12 +200,23 @@
     for copy in load_x + load_w:
         copy.start()
 
+    sources = [inbox_source(lat, lon, i // 4, i % 4) for i in range(8)]
+    barrier = pltpu.get_barrier_semaphore()
+
+    def tell(dlat, dlon):
+        pl.semaphore_signal(barrier, inc=1, device_id=(dlat, dlon), device_id_type=MESH)
+
+    due = jnp.int32(16)
+    for slat, slon, k in sources:
+        cross = (jnp.where((k & 2) != 0, slon, slon + LONS - 1) % 4) == 3
+        by = jnp.logical_and(cross, lat % 2 == 1)
+        slon = slon + jnp.where(by, jnp.where(slon % 4 == 3, -1, 1), 0)
+        pl.when(jnp.logical_not(same(slat, slon)))(functools.partial(tell, slat, slon))
     far = jnp.where(x >= 2, 1, 0)
     hosts = []
     for j in range(8):
         r, p, c = (j >> 1) & 1, j & 1, far if j < 4 else 1 - far
         hosts.append(((r * 2 + c) * 2 + p,) + block_host(lat, lon, r, c, p))
-    sources = [inbox_source(lat, lon, i // 4, i % 4) for i in range(8)]
     outer = lon + 2 * far - 1
     inner = lon + 1 - 2 * far
     relays = jnp.logical_or(x == 1, x == 2)
@@ -215,17 +225,6 @@
         hlat, hlon, pos, relayed = block_host(lat, jnp.where(relays, outer, lon), (j >> 1) & 1, far, j & 1)
         passed.append((jnp.logical_and(relays, relayed), hlat, hlon, pos))
 
-    barrier = pltpu.get_barrier_semaphore()
-
-    def tell(dlat, dlon):
-        pl.semaphore_signal(barrier, inc=1, device_id=(dlat, dlon), device_id_type=MESH)
-
-    due = jnp.int32(16)
-    for slat, slon, k in sources:
-        cross = (jnp.where((k & 2) != 0, slon, slon + LONS - 1) % 4) == 3
-        by = jnp.logical_and(cross, lat % 2 == 1)
-        slon = slon + jnp.where(by, jnp.where(slon % 4 == 3, -1, 1), 0)
-        pl.when(jnp.logical_not(same(slat, slon)))(functools.partial(tell, slat, slon))
     for j, (_, hlat, hlon, _, relayed) in enumerate(hosts):
         due = due + jnp.where(same(hlat, hlon), 0, 1)
     for flag, *_ in passed:
@@ -307,6 +306,7 @@
     for src, dst, rel, ss, rs, ts, us in halo:
         for j, (k, hlat, hlon, pos, relayed) in enumerate(hosts[:4]):
             pl.when(relayed)(lambda: relay_copy(src, rel, ss, ts, k, j).start())
+        for k, hlat, hlon, pos, relayed in hosts[:4]:
             pl.when(jnp.logical_not(relayed))(lambda: send(src, dst, ss, rs, k, hlat, hlon, pos))
     for src, dst, rel, ss, rs, ts, us in halo:
         for k, hlat, hlon, pos, _ in hosts[4:]:
@@ -345,26 +345,30 @@
             for s in range(2):
                 pl.when(slot == s)(functools.partial(go, s))
 
-    def a_copy():
+    def a_copy(part):
+        rows = pl.ds(2 * part, 2)
         return pltpu.make_async_remote_copy(
-            src_ref=a_src, dst_ref=a_dst, send_sem=a_sem.at[0], recv_sem=a_sem.at[1],
+            src_ref=a_src.at[rows], dst_ref=a_dst.at[rows], send_sem=a_sem.at[part], recv_sem=a_sem.at[4 + part],
             device_id=(zl * 2 + 1 - core, lon), device_id_type=MESH,
         )
 
     def core_to_plane():
-        a_copy().wait()
-        for x_ in range(4):
-            both = acc[2 * x_ : 2 * x_ + 2, core] + a_dst[2 * x_ : 2 * x_ + 2].astype(F32)
+        for dx in (2, 1, 3, 0):
+            x_ = x ^ dx
+            a_copy(x_).wait()
+            rows = pl.ds(2 * x_, 2)
+            both = acc[rows, core] + a_dst[rows].astype(F32)
             both = both.astype(BF).reshape(64, D)
             for y_ in range(4):
                 b_src[y_ * 4 + x_] = both[:, 128 * y_ : 128 * y_ + 128]
-
-        for d in FAR_FIRST:
-            partner = yx ^ d
-            pltpu.make_async_remote_copy(
-                src_ref=b_src.at[partner], dst_ref=b_dst.at[yx], send_sem=bs_sem.at[partner], recv_sem=br_sem.at[yx],
-                device_id=at(partner // 4, partner % 4, z, core), device_id_type=MESH,
-            ).start()
+            for dy in (2, 1, 3, 0):
+                if dx + dy:
+                    partner = (y ^ dy) * 4 + x_
+                    pltpu.make_async_remote_copy(
+                        src_ref=b_src.at[partner], dst_ref=b_dst.at[yx],
+                        send_sem=bs_sem.at[partner], recv_sem=br_sem.at[yx],
+                        device_id=at(y ^ dy, x_, z, core), device_id_type=MESH,
+                    ).start()
         b_dst[yx] = b_src[yx]
 
     def plane_to_ring():
@@ -421,8 +425,10 @@
     both_ctx = ctx[...].reshape(288, D)
     both_cot = cots[...].reshape(288, D)
     acc[...] = (dot(both_ctx, both_cot, 0, 0) * factor).reshape(8, 2, 32, D)
-    a_src[...] = acc[:, 1 - core].astype(BF)
-    a_copy().start()
+    for dx in (2, 1, 3, 0):
+        rows = pl.ds(2 * (x ^ dx), 2)
+        a_src[rows] = acc[rows, 1 - core].astype(BF)
+        a_copy(x ^ dx).start()
 
     gctx[...] = dot(both_cot, out_w[...], 1, 1).astype(BF).reshape(2, 144, D)
     core_to_plane()
@@ -567,7 +573,7 @@
         ]
         + [dma((8,))] * 8
         + [dma((4,))] * 4
-        + [dma((2,)), dma((16,)), dma((16,)), dma((4,)), dma((16,)), dma((4,)), dma, pltpu.SemaphoreType.REGULAR],
+        + [dma((8,)), dma((16,)), dma((16,)), dma((4,)), dma((16,)), dma((4,)), dma, pltpu.SemaphoreType.REGULAR],
         compiler_params=pltpu.CompilerParams(
             collective_id=0, has_side_effects=True, vmem_limit_bytes=VMEM_LIMIT
         ),

time: 52.7 us -> 52.1 us (0.989)
  Pallas kernels: 49.9 us -> 49.3 us
    pallas_call x1, Pallas kernels: 49.9 us -> 49.3 us  [on_device(): pl.pallas_call(functools.partial(kernel, factor), out_shape=[pltpu.VMEM((...]
where the time goes in v5:
time: 52.1 us; the launch traced here: 52 us
  Pallas kernels  49.3 us (95%)
  local copies, waits for them, and re-layouts  2.03 us (4%)
  between operations  0.64 us (1%)
    pallas_call x1, Pallas kernels, on_device(): pl.pallas_call(functools.partial(kernel, factor), out_shape=[pltpu.VMEM((...  49.3 us
    unnamed x3, local copies, waits for them, and re-layouts  2.03 us

profile of v5, /device:TPU:1, one launch (start us, length us, event | category | flops | bytes accessed | tf_op | source)
XLA Modules:
  0.0 52.0 jit_solution(5169362650754150961)
XLA Ops:
  0.6 49.3 %window_attention.1 = (bf16[72,4,512]{2,1,0:T(4,128)(2,1)S(1)}, bf16[72,4,512]{2,1,0:T(4,128)(2,1)S(1)}, f32[16,32]{1,0:T(8,128)S(1)}) custom-call(bf16[72,4,512]{2,1,0:T(4,128)(2,1)} %bitcast.16, bf16[512,1536]{1,0:T(8,128)(2,1)} %qkv_hbm.1, bf16[512,512]{1,0:T(8,128)(2,1)} %out_hbm.1, bf16[72,4,512]{2,1,0:T(4,128)(2,1)} %bitcast.17), custom_call_target="tpu_custom_call" | custom-call | flops 1600000000 | bytes 4000000 | tf_op jit(solution)/shard_map/window_attention/pallas_call | solution.py:535
  50.0 0.7 %copy.10 = bf16[4,6,12,512]{3,0,2,1:T(4,128)(2,1)} copy(bf16[4,6,12,512]{3,0,2,1:T(4,128)(2,1)S(1)} %bitcast.14) | data formatting | bytes 589824
  50.7 0.7 %copy.11 = bf16[4,6,12,512]{3,0,2,1:T(4,128)(2,1)} copy(bf16[4,6,12,512]{3,0,2,1:T(4,128)(2,1)S(1)} %bitcast.13) | data formatting | bytes 589824
  51.4 0.6 %copy.12 = f32[32,16]{0,1:T(8,128)} copy(f32[32,16]{0,1:T(8,128)S(1)} %bitcast.15) | data formatting | bytes 4096
